TPU v7x, 256 devices: a whole 4x4x8 slice. The times are simulated.
256 devices in a mesh: expert: 16 (over y_hi, z), hidden: 16 (over x, y_lo, core).
Axes of the slice: x: 4, y: 4 (y_hi: 2, y_lo: 2; y = y_hi * 2 + y_lo), z: 8, core: 2. Of those that a mesh axis runs over, the one named last changes fastest.
Arguments:
- tokens: bfloat16 [16384, 2048], P(('expert', 'hidden')), may hold values from -6 to 6
- cotangent: bfloat16 [16384, 2048], P(('expert', 'hidden')), may hold values from -6 to 6
- order: int32 [256, 64], P(('expert', 'hidden')), may hold values from 0 to 63, each once within a row
- w_in: bfloat16 [16, 2048, 8192], P('expert', None, 'hidden'), may hold values from -0.125 to 0.125
- w_out: bfloat16 [16, 8192, 2048], P('expert', 'hidden'), may hold values from -0.0625 to 0.0625
- gains: float32 [16, 2048], P('expert'), may hold values from 0.5 to 1.5
- centroids: float32 [16, 2048], P('expert'), may hold values from -0.125 to 0.125
- saved_pre: bfloat16 [16, 1024, 8192], P('expert', None, 'hidden'), may hold values from -6 to 6
- saved_out: bfloat16 [16, 1024, 2048], P('expert', 'hidden'), may hold values from -6 to 6
Outputs:
- grad_tokens: bfloat16 [16384, 2048], P(('expert', 'hidden'))
- grad_w_in: bfloat16 [16, 2048, 8192], P('expert', None, 'hidden')
- grad_w_out: bfloat16 [16, 8192, 2048], P('expert', 'hidden')
- grad_gains: float32 [16, 2048], P('expert')
- grad_centroids: float32 [16, 2048], P('expert')
Inputs may be any that keep to these rules, and one draw needn't show every extreme that they name: Each row of order is a permutation of 0 to 63, so each device assigns exactly 4 rows to each expert.
All inputs are finite; a program needn't handle non-finite values.
Results may differ from a plain program's by a relative error of at most 0.023.
Values may be sent and summed in bfloat16 or wider, within the bound.
A program may use at most 128 MiB of HBM per device.

v0:
```python
import jax
import jax.numpy as jnp
from jax import lax
from jax.sharding import PartitionSpec as P


def gelu_pair(value):
    result, pull = jax.vjp(lambda u: jax.nn.gelu(u, approximate=True), value)
    return (result, pull(jnp.ones_like(value))[0])


def inner_dot(left, right):
    return lax.dot_general(
        left, right, (((0,), (0,)), ((), ())), preferred_element_type=jnp.float32
    )


def outer_dot(left, right):
    return lax.dot_general(
        left, right, (((1,), (1,)), ((), ())), preferred_element_type=jnp.float32
    )


def prepare_inputs(rows, grads, norm_gain, expert_centroid):
    input_flat = rows.astype(jnp.float32)
    output_gradient_flat = grads.astype(jnp.float32)
    reciprocal_norm = lax.rsqrt(jnp.mean(input_flat * input_flat, axis=-1, keepdims=True) + 1e-06)
    normalized_input = input_flat * reciprocal_norm
    normalized_rows = (normalized_input * norm_gain).astype(jnp.bfloat16)
    gate_weight = jax.nn.sigmoid(jnp.sum(input_flat * expert_centroid, axis=-1))
    output_gradient_gated = (gate_weight[:, None] * output_gradient_flat).astype(jnp.bfloat16)
    return (
        input_flat,
        output_gradient_flat,
        reciprocal_norm,
        normalized_input,
        normalized_rows,
        gate_weight,
        output_gradient_gated,
    )


def shards(tokens, cotangent, order, w_in, w_out, gains, centroids, saved_pre, saved_out):
    tok_dev = tokens.shape[0]
    width = tokens.shape[1]
    expert_count = lax.axis_size("expert")
    per_expert = tok_dev // expert_count
    route = order[0]
    norm_gain = gains[0]
    expert_centroid = centroids[0]
    w_first = w_in[0]
    w_second = w_out[0]
    pre = saved_pre[0]
    zout = saved_out[0].astype(jnp.float32)
    x_slots = tokens[route].reshape(expert_count, per_expert, width)
    dy_slots = cotangent[route].reshape(expert_count, per_expert, width)
    x_recv, dy_recv = (
        lax.all_to_all(x_slots, "expert", split_axis=0, concat_axis=0, tiled=True),
        lax.all_to_all(dy_slots, "expert", split_axis=0, concat_axis=0, tiled=True),
    )
    (
        input_flat,
        output_gradient_flat,
        reciprocal_norm,
        normalized_input,
        normalized_rows,
        gate_weight,
        output_gradient_gated,
    ) = prepare_inputs(
        x_recv.reshape(tok_dev, width), dy_recv.reshape(tok_dev, width), norm_gain, expert_centroid
    )
    n_piece = lax.all_gather(normalized_rows, "hidden", axis=0, tiled=True)
    g_piece = lax.all_gather(output_gradient_gated, "hidden", axis=0, tiled=True)
    pre_piece = pre.astype(jnp.float32)
    act, slope = gelu_pair(pre_piece)
    act = act.astype(jnp.bfloat16)
    d_pre = (outer_dot(g_piece, w_second) * slope).astype(jnp.bfloat16)
    g_first = inner_dot(n_piece, d_pre)
    g_second = inner_dot(act, g_piece)
    g_first, g_second, d_pre_all = (g_first, g_second, d_pre)
    norm_gradient = lax.psum_scatter(
        outer_dot(d_pre_all, w_first).astype(jnp.bfloat16),
        "hidden",
        scatter_dimension=0,
        tiled=True,
    ).astype(jnp.float32)
    dgate = jnp.sum(output_gradient_flat * (input_flat + zout), axis=-1)
    logit_gradient = dgate * gate_weight * (1.0 - gate_weight)
    scaled_rows = norm_gradient * norm_gain
    input_gradient = (
        output_gradient_flat * (1.0 + gate_weight[:, None])
        + reciprocal_norm
        * (
            scaled_rows
            - normalized_input * jnp.mean(scaled_rows * normalized_input, axis=-1, keepdims=True)
        )
        + logit_gradient[:, None] * expert_centroid
    )
    input_gradient = input_gradient.astype(jnp.bfloat16)
    gain_gradient, g_cent = lax.psum(
        (
            jnp.sum(norm_gradient * normalized_input, axis=0),
            jnp.sum(logit_gradient[:, None] * input_flat, axis=0),
        ),
        "hidden",
    )
    returned = lax.all_to_all(
        input_gradient.reshape(expert_count, per_expert, width),
        "expert",
        split_axis=0,
        concat_axis=0,
        tiled=True,
    )
    grad_tokens = (
        jnp.zeros((tok_dev, width), jnp.bfloat16).at[route].set(returned.reshape(tok_dev, width))
    )
    return (
        grad_tokens,
        g_first.astype(jnp.bfloat16)[None],
        g_second.astype(jnp.bfloat16)[None],
        gain_gradient[None],
        g_cent[None],
    )


def solution(mesh):
    placed = (
        P(("expert", "hidden"), None),
        P(("expert", "hidden"), None),
        P(("expert", "hidden"), None),
        P("expert", None, "hidden"),
        P("expert", "hidden", None),
        P("expert", None),
        P("expert", None),
        P("expert", None, "hidden"),
        P("expert", "hidden", None),
    )
    return jax.shard_map(
        shards,
        mesh=mesh,
        in_specs=placed,
        out_specs=(
            P(("expert", "hidden"), None),
            P("expert", None, "hidden"),
            P("expert", "hidden", None),
            P("expert", None),
            P("expert", None),
        ),
        check_vma=False,
    )
```

profile of v0, /device:TPU:16, one launch (start us, length us, event | category | flops | bytes accessed | tf_op | source)
XLA Modules:
  0.0 257.6 jit_solution(4510144262093171978)
XLA Ops:
  7.2 0.0 copy-start
  7.2 0.0 copy-start.1
  7.2 0.8 fusion.33
  8.0 2.0 gather_fusion.1
  10.0 0.8 reshape.128
  10.8 0.0 copy-start.2
  10.8 11.6 %all-to-all-start.1 = ((bf16[16,4,2048]{2,1,0:T(4,128)(2,1)}), bf16[16,4,2048]{2,1,0:T(4,128)(2,1)S(1)}, u32[]{:S(2)}, u32[]{:S(2)}) async-start(bf16[16,4,2048]{2,1,0:T(4,128)(2,1)} %reshape.128), calls=%async_computation.1 | async-start | bytes 524288 | tf_op jit(solution)/shard_map/all_to_all | solution.py:58
  22.4 0.0 copy-done.1
  22.4 0.0 copy-start.3
  22.4 0.7 gather_fusion
  23.1 0.8 reshape.127
  24.0 7.9 %all-to-all-done.1 = bf16[16,4,2048]{2,1,0:T(4,128)(2,1)S(1)} async-done(((bf16[16,4,2048]{2,1,0:T(4,128)(2,1)}), bf16[16,4,2048]{2,1,0:T(4,128)(2,1)S(1)}, u32[]{:S(2)}, u32[]{:S(2)}) %all-to-all-start.1) | async-done | bytes 262176 | tf_op jit(solution)/shard_map/all_to_all | solution.py:58
  31.8 6.7 %all-to-all-start = ((bf16[16,4,2048]{2,1,0:T(4,128)(2,1)}), bf16[16,4,2048]{2,1,0:T(4,128)(2,1)S(1)}, u32[]{:S(2)}, u32[]{:S(2)}) async-start(bf16[16,4,2048]{2,1,0:T(4,128)(2,1)} %reshape.127), calls=%async_computation | async-start | bytes 524288 | tf_op jit(solution)/shard_map/all_to_all | solution.py:59
  38.5 0.0 all-gather.3.cloned.1.call-start
  38.6 0.0 copy-done.2
  38.6 0.2 reshape.134
  38.7 8.8 %all-to-all-done = bf16[16,4,2048]{2,1,0:T(4,128)(2,1)S(1)} async-done(((bf16[16,4,2048]{2,1,0:T(4,128)(2,1)}), bf16[16,4,2048]{2,1,0:T(4,128)(2,1)S(1)}, u32[]{:S(2)}, u32[]{:S(2)}) %all-to-all-start) | async-done | bytes 262176 | tf_op jit(solution)/shard_map/all_to_all | solution.py:59
  47.5 0.0 copy-done.3
  47.5 0.4 multiply_reduce_fusion.1
  48.0 0.1 div.24
  48.1 0.8 multiply_convert_fusion.1
  48.9 0.0 all-gather.3.cloned.1.call-update
  48.9 0.0 reduce-scatter.2.cloned.1.call-start
  49.0 37.7 %all-gather.3.cloned.1.call-done = bf16[1024,2048]{1,0:T(8,128)(2,1)} async-done(((bf16[64,2048]{1,0:T(8,128)(2,1)}), bf16[1024,2048]{1,0:T(8,128)(2,1)}) %all-gather.3.cloned.1.call-update) | async-done | bytes 4194320 | tf_op jit(solution)/shard_map/all_gather | solution.py:73
  86.7 6.5 %fusion.6 = bf16[1024,512]{1,0:T(8,128)(2,1)S(1)} fusion(bf16[1024,2048]{1,0:T(8,128)(2,1)} %all-gather.3.cloned.1.call-done, bf16[1,512,2048]{2,1,0:T(8,128)(2,1)} %param.13, bf16[1,1024,512]{2,1,0:T(8,128)(2,1)} %param.16), kind=kOutput, calls=%fused_computation.17 | convolution fusion | flops 2157969408 | bytes 8388608 | tf_op jit(solution)/shard_map/dot_general | solution.py:19
  93.2 0.0 copy-start.5
  93.2 1.0 copy-done.5
  94.2 0.0 copy-done
  94.2 4.4 %convolution_convert_fusion = bf16[1024,2048]{1,0:T(8,128)(2,1)} fusion(bf16[1024,512]{1,0:T(8,128)(2,1)S(1)} %fusion.6, bf16[1,2048,512]{2,1,0:T(8,128)(2,1)S(1)} %copy-done), kind=kOutput, calls=%fused_computation.8 | convolution fusion | flops 2149580800 | bytes 7340032 | tf_op jit(solution)/shard_map/dot_general | solution.py:19
  98.6 0.0 copy-start.4
  98.6 0.0 reduce-scatter.2.cloned.1.call-update
  98.6 0.0 all-gather.5.cloned.1.call-start
  98.7 0.3 multiply_reduce_fusion
  99.0 0.1 rsqrt.12
  99.1 69.8 %reduce-scatter.2.cloned.1.call-done = bf16[64,2048]{1,0:T(8,128)(2,1)} async-done(((bf16[1024,2048]{1,0:T(8,128)(2,1)}), bf16[64,2048]{1,0:T(8,128)(2,1)}) %reduce-scatter.2.cloned.1.call-update) | async-done | bytes 262160 | tf_op jit(solution)/shard_map/reduce_scatter | solution.py:81
  168.9 0.0 copy-done.4
  168.9 2.0 fusion.30
  170.9 0.0 all-gather.5.cloned.1.call-update
  170.9 0.1 reduce_sum.60
  171.0 1.2 fusion.29
  172.2 0.8 reshape.129
  173.1 9.9 %all-to-all-start.2 = ((bf16[16,4,2048]{2,1,0:T(4,128)(2,1)}), bf16[16,4,2048]{2,1,0:T(4,128)(2,1)S(1)}, u32[]{:S(2)}, u32[]{:S(2)}) async-start(bf16[16,4,2048]{2,1,0:T(4,128)(2,1)} %reshape.129), calls=%async_computation.3 | async-start | bytes 524288 | tf_op jit(solution)/shard_map/all_to_all | solution.py:107
  183.0 6.4 %fusion.2 = bf16[1,512,2048]{2,1,0:T(8,128)(2,1)} fusion(bf16[1024,2048]{1,0:T(8,128)(2,1)} %all-gather.3.cloned.1.call-done, bf16[1,1024,512]{2,1,0:T(8,128)(2,1)} %param.16), kind=kOutput, calls=%fused_computation.13 | convolution fusion | flops 2153775104 | bytes 7340032 | tf_op jit(solution)/shard_map/dot_general | solution.py:13
  189.4 53.8 %all-reduce = (f32[1,2048]{1,0:T(1,128)}, f32[1,2048]{1,0:T(1,128)}) all-reduce(f32[1,2048]{1,0:T(1,128)S(1)} %bitcast.37, f32[1,2048]{1,0:T(1,128)S(1)} %bitcast.38), channel_id=1, replica_groups=mesh['expert'=16,'hidden'=16] {'hidden'}, use_global_device_ids=true, to_apply=%region_7.0 | all-reduce | flops 4096 | bytes 32768 | tf_op jit(solution)/shard_map/psum | solution.py:100
  243.2 0.0 all-to-all-done.2
  243.2 0.1 reshape.155
  243.3 1.7 scatter_custom_fusion
  244.9 0.0 all-gather.5.cloned.1.call-done
  244.9 6.2 %fusion.1 = bf16[1,2048,512]{2,1,0:T(8,128)(2,1)} fusion(bf16[1024,2048]{1,0:T(8,128)(2,1)} %all-gather.5.cloned.1.call-done, bf16[1024,512]{1,0:T(8,128)(2,1)} %copy-done.5), kind=kOutput, calls=%fused_computation.12 | convolution fusion | flops 2148532224 | bytes 7340032 | tf_op jit(solution)/shard_map/dot_general | solution.py:13
  (7 shorter events, 0.1 us)
Async XLA Ops:
  7.2 87.1 %copy-start = (bf16[1,2048,512]{2,1,0:T(8,128)(2,1)S(1)}, bf16[1,2048,512]{2,1,0:T(8,128)(2,1)}, u32[]{:S(2)}) copy-start(bf16[1,2048,512]{2,1,0:T(8,128)(2,1)} %param.12) | copy-start | bytes 6291460
  7.2 15.2 %copy-start.1 = (bf16[64,2048]{1,0:T(8,128)(2,1)S(1)}, bf16[64,2048]{1,0:T(8,128)(2,1)}, u32[]{:S(2)}) copy-start(bf16[64,2048]{1,0:T(8,128)(2,1)} %param.10) | copy-start | bytes 786436
  10.8 27.8 %copy-start.2 = (bf16[1,64,2048]{2,1,0:T(8,128)(2,1)S(1)}, bf16[1,64,2048]{2,1,0:T(8,128)(2,1)}, u32[]{:S(2)}) copy-start(bf16[1,64,2048]{2,1,0:T(8,128)(2,1)} %param.17) | copy-start | bytes 786436
  10.8 21.0 %all-to-all-start.1 = ((bf16[16,4,2048]{2,1,0:T(4,128)(2,1)}), bf16[16,4,2048]{2,1,0:T(4,128)(2,1)S(1)}, u32[]{:S(2)}, u32[]{:S(2)}) async-start(bf16[16,4,2048]{2,1,0:T(4,128)(2,1)} %reshape.128), calls=%async_computation.1 | async-start | bytes 524288 | tf_op jit(solution)/shard_map/all_to_all | solution.py:58
  22.4 25.1 %copy-start.3 = (f32[1,2048]{1,0:T(1,128)S(1)}, f32[1,2048]{1,0:T(1,128)}, u32[]{:S(2)}) copy-start(f32[1,2048]{1,0:T(1,128)} %param.15) | copy-start | bytes 24580
  31.8 15.7 %all-to-all-start = ((bf16[16,4,2048]{2,1,0:T(4,128)(2,1)}), bf16[16,4,2048]{2,1,0:T(4,128)(2,1)S(1)}, u32[]{:S(2)}, u32[]{:S(2)}) async-start(bf16[16,4,2048]{2,1,0:T(4,128)(2,1)} %reshape.127), calls=%async_computation | async-start | bytes 524288 | tf_op jit(solution)/shard_map/all_to_all | solution.py:59
  38.5 48.2 %all-gather.3.cloned.1.call-start = ((), (), s32[]{:S(2)}) async-start(), calls=%async_computation.4 | async-start | bytes 4456448 | tf_op jit(solution)/shard_map/all_gather | solution.py:73
  48.9 120.0 %reduce-scatter.2.cloned.1.call-start = ((), (), s32[]{:S(2)}) async-start(), calls=%async_computation.5 | async-start | bytes 4456448 | tf_op jit(solution)/shard_map/reduce_scatter | solution.py:81
  93.2 1.0 copy-start.5
  98.6 70.3 %copy-start.4 = (f32[1,2048]{1,0:T(1,128)S(1)}, f32[1,2048]{1,0:T(1,128)}, u32[]{:S(2)}) copy-start(f32[1,2048]{1,0:T(1,128)} %param.14) | copy-start | bytes 24580
  98.6 146.3 %all-gather.5.cloned.1.call-start = ((), (), s32[]{:S(2)}) async-start(), calls=%async_computation.6 | async-start | bytes 4456448 | tf_op jit(solution)/shard_map/all_gather | solution.py:72
  173.1 70.1 %all-to-all-start.2 = ((bf16[16,4,2048]{2,1,0:T(4,128)(2,1)}), bf16[16,4,2048]{2,1,0:T(4,128)(2,1)S(1)}, u32[]{:S(2)}, u32[]{:S(2)}) async-start(bf16[16,4,2048]{2,1,0:T(4,128)(2,1)} %reshape.129), calls=%async_computation.3 | async-start | bytes 524288 | tf_op jit(solution)/shard_map/all_to_all | solution.py:107
Sparse Core Ops, SparseCore 0:
  49.1 37.5 all-gather.2
  98.8 70.0 reduce-scatter.1
  171.3 40.2 all-gather.4
where the time goes:
time: 258 us
  waiting for transfers between devices  124 us (48%)
  blocking collectives  53.8 us (21%)
  starting transfers between devices  28.3 us (11%)
  matrix products  23.4 us (9%)
  between operations  13.9 us (5%)
  local copies, waits for them, and re-layouts  8.42 us (3%)
  other arithmetic  5.55 us (2%)
    reduce_scatter x1, waiting for transfers between devices, shards(): lax.psum_scatter(outer_dot(d_pre_all, w_first).astype(jnp.bfloat16), 'hid...  69.8 us
    psum x1, blocking collectives, shards(): lax.psum((jnp.sum(norm_gradient * normalized_input, axis=0), jnp.sum(logi...  53.8 us
    all_gather x1, waiting for transfers between devices, shards(): lax.all_gather(output_gradient_gated, 'hidden', axis=0, tiled=True)  37.7 us
    dot_general x2, matrix products, inner_dot(): lax.dot_general(left, right, (((0,), (0,)), ((), ())), preferred_element_...  12.6 us
    all_to_all x1, starting transfers between devices, shards(): lax.all_to_all(x_slots, 'expert', split_axis=0, concat_axis=0, tiled=True)  11.6 us
    dot_general x2, matrix products, outer_dot(): lax.dot_general(left, right, (((1,), (1,)), ((), ())), preferred_element_...  10.9 us
    all_to_all x1, starting transfers between devices, shards(): lax.all_to_all(input_gradient.reshape(expert_count, per_expert, width), '...  9.94 us
    all_to_all x1, waiting for transfers between devices, shards(): lax.all_to_all(dy_slots, 'expert', split_axis=0, concat_axis=0, tiled=True)  8.76 us
  transfers between devices with their start and end apart: 6, of which 4 were waited for; matrix products, arithmetic and copies ran while one was open for 5% of the time, Pallas kernels for 0%

commit v1 on v0

v1 whole, which is shorter than its diff:
```python
import functools

import jax
import jax.numpy as jnp
from jax import lax
from jax.experimental import pallas as pl
from jax.experimental.pallas import tpu as pltpu
from jax.sharding import PartitionSpec as P

MESH = pl.DeviceIdType.MESH
F32 = jnp.float32
BF16 = jnp.bfloat16
N = 16
ROWS = 64
D = 2048
FD = 512
CH = 512
HALF = 32


def dot_nn(a, b):
    return jnp.dot(a, b, preferred_element_type=F32)


def dot_nt(a, b):
    return lax.dot_general(a, b, (((1,), (1,)), ((), ())), preferred_element_type=F32)


def dot_tn(a, b):
    return lax.dot_general(a, b, (((0,), (0,)), ((), ())), preferred_element_type=F32)


def iota(shape, dim):
    return lax.broadcasted_iota(jnp.int32, shape, dim)


def onehot(mask):
    return jnp.where(mask, 1.0, 0.0).astype(BF16)


def chunk_pick(c, rows_first):
    shape = (ROWS, 256) if rows_first else (256, ROWS)
    k = iota(shape, 0 if rows_first else 1)
    q = iota(shape, 1 if rows_first else 0)
    return onehot(q == ((k >> 2) << 4) + 4 * c + (k & 3))


def gelu_pair(v):
    k0, k1 = 0.7978845608028654, 0.044715
    v2 = v * v
    t = jnp.tanh(k0 * (v + k1 * v2 * v))
    a = 0.5 * v * (1.0 + t)
    g = 0.5 * (1.0 + t) + 0.5 * v * (1.0 - t * t) * (k0 * (1.0 + 3.0 * k1 * v2))
    return a, g


def kernel(
    tok, cot, order, win_h, wout_h, gains, cent, pre_h, zout_h,
    gt_o, gwi_o, gwo_o, gg_o, gc_o,
    win, wout, pre, zout, act, slope, dh, dh2,
    a_dy, a_x, r_dy, r_x, dy, x, part, rc, fa, fb, fc, fr1, fr2, stat, vec, dxs, rb, stage_i, stage_o,
    load_sem, a2a_s, a2a_r, stat_s, stat_r, vec_s, vec_r, ret_s, ret_r, ag_s, ag_r, rs_s, rs_r, out_sem,
):
    e = lax.axis_index("expert")
    h = lax.axis_index("hidden")
    xi = h // 4
    yc = h % 4
    yi = yc // 2
    ci = yc % 2
    yo = 1 - yi
    co = 1 - ci
    yoc = 2 * yo + ci
    xp, xm = (h + 4) % N, (h + 12) % N
    yn = h + 2 * (yo - yi)
    cn = h + co - ci

    barrier = pltpu.get_barrier_semaphore()

    @pl.loop(1, N)
    def _(i):
        pl.semaphore_signal(barrier, 1, device_id={"expert": (e + i) % N, "hidden": h}, device_id_type=MESH)
        pl.semaphore_signal(barrier, 1, device_id={"expert": e, "hidden": (h + i) % N}, device_id_type=MESH)

    loads = [
        pltpu.make_async_copy(pre_h.at[0, pl.ds(pl.multiple_of(((xi + k) % 4) * 256, 256), 256)], pre.at[k], load_sem.at[k])
        for k in range(4)
    ]
    loads.append(pltpu.make_async_copy(zout_h.at[0], zout, load_sem.at[4]))
    loads.append(pltpu.make_async_copy(wout_h.at[0], wout, load_sem.at[5]))
    loads.append(pltpu.make_async_copy(win_h.at[0], win, load_sem.at[6]))
    for c in loads:
        c.start()

    to_slot = onehot(iota((ROWS, ROWS), 0) == order[...])
    q = iota((256, ROWS), 0)
    spread = onehot(iota((256, ROWS), 1) == ((q >> 4) << 2) + (q & 3))
    pick = dot_nt(spread, to_slot)
    chunk_of = (q >> 2) & 3
    picks = [jnp.where(chunk_of == c, pick, 0.0).astype(BF16) for c in range(4)]

    def dispatch(src, dst):
        acc = dot_nn(picks[0], src[:, 0:CH])
        for c in range(1, 4):
            acc += dot_nn(picks[c], src[:, c * CH : (c + 1) * CH])
        dst[...] = acc.astype(BF16).reshape(N, 16, CH)

    def a2a_copy(src, dst, ssem, rsem, i):
        return pltpu.make_async_remote_copy(
            src_ref=src.at[(e + i) % N], dst_ref=dst.at[e], send_sem=ssem, recv_sem=rsem,
            device_id={"expert": (e + i) % N, "hidden": h}, device_id_type=MESH,
        )

    def a2a_start(t, src, dst):
        @pl.loop(1, N)
        def _(i):
            a2a_copy(src, dst, a2a_s.at[t, i], a2a_r.at[t, i], i).start()

        dst[e] = src[e]

    def a2a_arrived(t, src, dst):
        @pl.loop(1, N)
        def _(i):
            pltpu.make_async_remote_copy(
                src_ref=src.at[(e + i) % N], dst_ref=dst.at[(e + N - i) % N], send_sem=a2a_s.at[t, i], recv_sem=a2a_r.at[t, i],
                device_id={"expert": (e + i) % N, "hidden": h}, device_id_type=MESH,
            ).wait()

    dispatch(cot, a_dy)
    pl.semaphore_wait(barrier, 2 * (N - 1))
    a2a_start(0, a_dy, r_dy)
    dispatch(tok, a_x)
    a2a_start(1, a_x, r_x)

    for k in range(4):
        loads[k].wait()

    @pl.loop(0, 16)
    def _(i):
        k, rows = i // 4, pl.ds(pl.multiple_of((i % 4) * 64, 64), 64)
        a, g = gelu_pair(pre[k, rows].astype(F32))
        act[k, rows] = a.astype(BF16)
        slope[k, rows] = g

    def remote(sems, i, src, dst, where):
        return pltpu.make_async_remote_copy(
            src_ref=src, dst_ref=dst, send_sem=sems[0].at[i], recv_sem=sems[1].at[i],
            device_id={"expert": e, "hidden": where}, device_id_type=MESH,
        )

    def gather_plan(t, buf):
        sems = (ag_s.at[t], ag_r.at[t])
        lo, hi = pl.ds(0, HALF), pl.ds(HALF, HALF)
        plan = {
            "own_xp": (buf.at[0, yc], buf.at[3, yc], xp, buf.at[3, yc]),
            "own_xm": (buf.at[0, yc], buf.at[1, yc], xm, buf.at[1, yc]),
            "own_y": (buf.at[0, yc], buf.at[0, yc], yn, buf.at[0, yoc]),
            "half_xp": (buf.at[3, yc, lo], buf.at[2, yc, lo], xp, buf.at[2, yc, lo]),
            "half_xm": (buf.at[1, yc, hi], buf.at[2, yc, hi], xm, buf.at[2, yc, hi]),
            "oy_xp": (buf.at[0, yoc], buf.at[3, yoc], xp, buf.at[3, yoc]),
            "oy_xm": (buf.at[0, yoc], buf.at[1, yoc], xm, buf.at[1, yoc]),
            "far_y": (buf.at[2, yc], buf.at[2, yc], yn, buf.at[2, yoc]),
        }
        for k in range(4):
            plan["core_%d" % k] = (buf.at[k, yc], buf.at[k, yc], cn, buf.at[k, 2 * yi + co])
            plan["core_y%d" % k] = (buf.at[k, yoc], buf.at[k, yoc], cn, buf.at[k, 2 * yo + co])
        out = {}
        for i, (name, (src, dst, where, got)) in enumerate(plan.items()):
            out[name] = (remote(sems, i, src, dst, where), remote(sems, i, src, got, where))
        return out

    class Gather:
        def __init__(self, t, buf):
            self.plan = gather_plan(t, buf)

        def start(self, *names):
            for n in names:
                self.plan[n][0].start()

        def got(self, *names):
            for n in names:
                self.plan[n][1].wait_recv()

        def sent(self, *names):
            for n in names:
                self.plan[n][0].wait_send()

        def sent_all(self):
            self.sent(*self.plan)

    def collect(src, dst):
        rows = src[...].reshape(256, CH)
        for c in range(4):
            dst[0, yc, :, c * CH : (c + 1) * CH] = dot_nn(chunk_pick(c, True), rows).astype(BF16)

    gd = Gather(0, dy)
    gx = Gather(1, x)

    a2a_arrived(0, a_dy, r_dy)
    collect(r_dy, dy)
    gd.start("own_xp", "own_xm", "own_y", "core_0")

    a2a_arrived(1, a_x, r_x)
    collect(r_x, x)

    loads[4].wait()
    xf = x[0, yc].astype(F32)
    dyf = dy[0, yc].astype(F32)
    r = lax.rsqrt(jnp.sum(xf * xf, axis=1, keepdims=True) * (1.0 / D) + 1e-06)
    s = jax.nn.sigmoid(jnp.sum(xf * cent[...], axis=1, keepdims=True))
    ds = jnp.sum(dyf * (xf + zout[...].astype(F32)), axis=1, keepdims=True)
    dlogit = ds * s * (1.0 - s)
    row_i, lane_i = iota((ROWS, 128), 0), iota((ROWS, 128), 1)
    s_mask, r_mask = lane_i == row_i, lane_i == row_i + ROWS
    stat[0, yc] = jnp.sum(jnp.where(s_mask, s, 0.0) + jnp.where(r_mask, r, 0.0), axis=0, keepdims=True)
    vec[h, 1:2] = jnp.sum(dlogit * xf, axis=0, keepdims=True)

    def stat_copy(i, got):
        to, frm = (h + i) % N, (h + N - i) % N
        slot = ((frm // 4 + 4 - xi) % 4, frm % 4) if got else ((xi + 4 - to // 4) % 4, yc)
        return pltpu.make_async_remote_copy(
            src_ref=stat.at[0, yc], dst_ref=stat.at[slot[0], slot[1]], send_sem=stat_s.at[i], recv_sem=stat_r.at[i],
            device_id={"expert": e, "hidden": to}, device_id_type=MESH,
        )

    @pl.loop(1, N)
    def _(i):
        stat_copy(i, False).start()

    gd.got("own_xp", "own_xm", "own_y")
    gd.start("half_xp", "half_xm", "oy_xp", "oy_xm", "core_1", "core_3", "core_y0")

    @pl.loop(1, N)
    def _(i):
        stat_copy(i, True).wait()

    loads[5].wait()
    loads[6].wait()

    def forward(k):
        acc = [dot_nt(dy[k].reshape(256, D), wout[f * 256 : (f + 1) * 256]) for f in range(2)]
        for j in range(4):
            rows = slice(j * ROWS, (j + 1) * ROWS)
            line = stat[k, j]
            sj = jnp.sum(jnp.where(s_mask, line, 0.0), axis=1, keepdims=True)
            rj = jnp.sum(jnp.where(r_mask, line, 0.0), axis=1, keepdims=True)
            for f in range(2):
                cols = slice(f * 256, (f + 1) * 256)
                v = acc[f][rows] * (slope[k, rows, cols] * sj)
                dh[k, rows, cols] = v.astype(BF16)
                dh2[k, rows, cols] = (v * rj).astype(BF16)
                act[k, rows, cols] = (act[k, rows, cols].astype(F32) * sj).astype(BF16)

        @pl.loop(0, 8)
        def _(n):
            cols = pl.ds(pl.multiple_of(n * 256, 256), 256)
            t = dot_nt(dh[k], win[cols]).astype(BF16)
            for j in range(4):
                part[j % 2, k, j // 2, :, cols] = t[j * ROWS : (j + 1) * ROWS]

    rs_sems = (rs_s, rs_r)
    core_rs = [remote(rs_sems, k, part.at[co, k], rc.at[k], cn) for k in range(4)]

    gd.got("core_0", "core_y0")
    forward(0)
    core_rs[0].start()
    gd.got("half_xp", "half_xm")
    gd.start("far_y", "core_2")
    gd.got("oy_xp", "oy_xm")
    gd.start("core_y1", "core_y3")
    gd.got("far_y")
    gd.start("core_y2")
    gx.start("own_xp", "own_xm", "own_y", "core_0")
    gd.got("core_1", "core_y1")
    forward(1)
    core_rs[1].start()
    gd.got("core_3", "core_y3")
    forward(3)
    core_rs[3].start()
    gd.got("core_2", "core_y2")
    forward(2)
    core_rs[2].start()

    def add(dst, *others):
        total = dst[...].astype(F32)
        for o in others:
            total += o[...].astype(F32)
        dst[...] = total.astype(BF16)

    def both_cores(k):
        core_rs[k].wait_recv()
        add(part.at[ci, k], rc.at[k])

    rs = {
        "a_p": remote(rs_sems, 4, part.at[ci, 1, yo], fa.at[0], xp),
        "a_m": remote(rs_sems, 5, part.at[ci, 3, yo], fa.at[1], xm),
        "r1": remote(rs_sems, 6, part.at[ci, 2, yo], fr1, yn),
        "b_p": remote(rs_sems, 7, part.at[ci, 2, yi, pl.ds(0, HALF)], fb.at[0], xp),
        "b_m": remote(rs_sems, 8, part.at[ci, 2, yi, pl.ds(HALF, HALF)], fb.at[1], xm),
        "r2": remote(rs_sems, 9, part.at[ci, 0, yo], fr2, yn),
        "c_p": remote(rs_sems, 10, part.at[ci, 1, yi], fc.at[0], xp),
        "c_m": remote(rs_sems, 11, part.at[ci, 3, yi], fc.at[1], xm),
    }
    both_cores(1)
    rs["a_p"].start()
    both_cores(3)
    rs["a_m"].start()
    both_cores(2)
    rs["r1"].start()
    both_cores(0)
    gx.got("own_xp", "own_xm", "own_y")
    gx.start("half_xp", "half_xm", "core_1", "core_3", "core_y0")

    out_copies = []

    def weight_out(n):
        cols = slice(n * 512, (n + 1) * 512)
        stage_o[:, cols] = dot_tn(
            act[...].reshape(N * ROWS, FD), dy[:, :, :, cols].reshape(N * ROWS, 512)
        ).astype(BF16)

    for n in range(4):
        weight_out(n)
    out_copies.append(pltpu.make_async_copy(stage_o, gwo_o.at[0], out_sem.at[0]))
    out_copies[-1].start()

    rs["r1"].wait_recv()
    add(part.at[ci, 2, yi], fr1)
    rs["b_p"].start()
    rs["b_m"].start()
    rs["a_p"].wait_recv()
    rs["a_m"].wait_recv()
    add(part.at[ci, 0, yo], fa.at[0], fa.at[1])
    rs["r2"].start()
    rs["b_p"].wait_recv()
    add(part.at[ci, 1, yi, pl.ds(0, HALF)], fb.at[0])
    rs["c_p"].start()
    rs["b_m"].wait_recv()
    add(part.at[ci, 3, yi, pl.ds(HALF, HALF)], fb.at[1])
    rs["c_m"].start()
    gx.start("oy_xp", "oy_xm")
    gx.got("half_xp", "half_xm")
    gx.start("far_y", "core_2")

    rs["r2"].wait_recv()
    rs["c_p"].wait_recv()
    rs["c_m"].wait_recv()
    dn = (
        part[ci, 0, yi].astype(F32) + fr2[...].astype(F32) + fc[0].astype(F32) + fc[1].astype(F32)
    )
    xf = x[0, yc].astype(F32)
    dyf = dy[0, yc].astype(F32)
    xhat = xf * r
    vec[h, 0:1] = jnp.sum(dn * xhat, axis=0, keepdims=True)
    qv = dn * gains[...]
    m = jnp.sum(qv * xhat, axis=1, keepdims=True) * (1.0 / D)
    dx = (dyf * (1.0 + s) + r * (qv - xhat * m) + dlogit * cent[...]).astype(BF16)
    acc = dot_nn(chunk_pick(0, False), dx[:, 0:CH])
    for c in range(1, 4):
        acc += dot_nn(chunk_pick(c, False), dx[:, c * CH : (c + 1) * CH])
    dxs[...] = acc.astype(BF16).reshape(N, 16, CH)

    def ret_copy(i, got):
        return pltpu.make_async_remote_copy(
            src_ref=dxs.at[(e + i) % N], dst_ref=rb.at[(e + N - i) % N if got else e],
            send_sem=ret_s.at[i], recv_sem=ret_r.at[i],
            device_id={"expert": (e + i) % N, "hidden": h}, device_id_type=MESH,
        )

    def vec_copy(i, got):
        return pltpu.make_async_remote_copy(
            src_ref=vec.at[h], dst_ref=vec.at[(h + N - i) % N if got else h], send_sem=vec_s.at[i], recv_sem=vec_r.at[i],
            device_id={"expert": e, "hidden": (h + i) % N}, device_id_type=MESH,
        )

    @pl.loop(1, N)
    def _(i):
        ret_copy(i, False).start()

    @pl.loop(1, N)
    def _(i):
        vec_copy(i, False).start()

    rb[e] = dxs[e]

    gx.got("oy_xp", "oy_xm")
    gx.start("core_y1", "core_y3")
    gx.got("far_y")
    gx.start("core_y2")
    gx.got(*["core_%d" % k for k in range(4)], *["core_y%d" % k for k in range(4)])

    eye = iota((256, 256), 0) == iota((256, 256), 1)
    for n in range(8):
        cols = slice(n * 256, (n + 1) * 256)
        gain = jnp.sum(jnp.where(eye, gains[:, cols], 0.0), axis=1, keepdims=True)
        t = dot_tn(x[:, :, :, cols].reshape(N * ROWS, 256), dh2[...].reshape(N * ROWS, FD))
        stage_i[cols] = (t * gain).astype(BF16)
    out_copies.append(pltpu.make_async_copy(stage_i, gwi_o.at[0], out_sem.at[1]))
    out_copies[-1].start()

    @pl.loop(1, N)
    def _(i):
        ret_copy(i, True).wait()
        vec_copy(i, True).wait()

    back = rb[...].reshape(256, CH)
    slot_of = dot_nt(to_slot, spread)
    q2 = iota((ROWS, 256), 1)
    for c in range(4):
        w = jnp.where(((q2 >> 2) & 3) == c, slot_of, 0.0).astype(BF16)
        gt_o[:, c * CH : (c + 1) * CH] = dot_nn(w, back).astype(BF16)
    total = vec[0]
    for i in range(1, N):
        total += vec[i]
    gg_o[...] = total[0:1]
    gc_o[...] = total[1:2]

    gd.sent_all()
    gx.sent_all()
    for c in core_rs:
        c.wait_send()
    for c in rs.values():
        c.wait_send()
    for c in out_copies:
        c.wait()


def shards(*args):
    vm = pl.BlockSpec(memory_space=pltpu.VMEM)
    hbm = pl.BlockSpec(memory_space=pl.ANY)
    rows4 = (4, 4, ROWS, D)
    dma = pltpu.SemaphoreType.DMA
    return pl.pallas_call(
        kernel,
        out_shape=(
            jax.ShapeDtypeStruct((ROWS, D), BF16),
            jax.ShapeDtypeStruct((1, D, FD), BF16),
            jax.ShapeDtypeStruct((1, FD, D), BF16),
            jax.ShapeDtypeStruct((1, D), F32),
            jax.ShapeDtypeStruct((1, D), F32),
        ),
        in_specs=[vm, vm, vm, hbm, hbm, vm, vm, hbm, hbm],
        out_specs=(vm, hbm, hbm, vm, vm),
        scratch_shapes=[
            pltpu.VMEM((D, FD), BF16),
            pltpu.VMEM((FD, D), BF16),
            pltpu.VMEM((4, 256, FD), BF16),
            pltpu.VMEM((ROWS, D), BF16),
            pltpu.VMEM((4, 256, FD), BF16),
            pltpu.VMEM((4, 256, FD), F32),
            pltpu.VMEM((4, 256, FD), BF16),
            pltpu.VMEM((4, 256, FD), BF16),
            pltpu.VMEM((N, 16, CH), BF16),
            pltpu.VMEM((N, 16, CH), BF16),
            pltpu.VMEM((N, 16, CH), BF16),
            pltpu.VMEM((N, 16, CH), BF16),
            pltpu.VMEM(rows4, BF16),
            pltpu.VMEM(rows4, BF16),
            pltpu.VMEM((2, 4, 2, ROWS, D), BF16),
            pltpu.VMEM((4, 2, ROWS, D), BF16),
            pltpu.VMEM((2, ROWS, D), BF16),
            pltpu.VMEM((2, HALF, D), BF16),
            pltpu.VMEM((2, ROWS, D), BF16),
            pltpu.VMEM((ROWS, D), BF16),
            pltpu.VMEM((ROWS, D), BF16),
            pltpu.VMEM((4, 4, 1, 128), F32),
            pltpu.VMEM((N, 2, D), F32),
            pltpu.VMEM((N, 16, CH), BF16),
            pltpu.VMEM((N, 16, CH), BF16),
            pltpu.VMEM((D, FD), BF16),
            pltpu.VMEM((FD, D), BF16),
            dma((7,)),
            dma((2, N)), dma((2, N)),
            dma((N,)), dma((N,)),
            dma((N,)), dma((N,)),
            dma((N,)), dma((N,)),
            dma((2, 16)), dma((2, 16)),
            dma((12,)), dma((12,)),
            dma((2,)),
        ],
        compiler_params=pltpu.CompilerParams(
            collective_id=0, has_side_effects=True, vmem_limit_bytes=56 * 2**20
        ),
    )(*args)


def solution(mesh):
    placed = (
        P(("expert", "hidden"), None),
        P(("expert", "hidden"), None),
        P(("expert", "hidden"), None),
        P("expert", None, "hidden"),
        P("expert", "hidden", None),
        P("expert", None),
        P("expert", None),
        P("expert", None, "hidden"),
        P("expert", "hidden", None),
    )
    return jax.shard_map(
        shards,
        mesh=mesh,
        in_specs=placed,
        out_specs=(
            P(("expert", "hidden"), None),
            P("expert", None, "hidden"),
            P("expert", "hidden", None),
            P("expert", None),
            P("expert", None),
        ),
        check_vma=False,
    )
```

time: 258 us -> 94.2 us (0.37)
  the two profiles are of different devices: /device:TPU:16 before, /device:TPU:6 now
where the time goes in v1:
time: 94.2 us; the launch traced here: 93.4 us
  Pallas kernels  85.4 us (91%)
  local copies, waits for them, and re-layouts  7.39 us (8%)
    pallas_call x1, Pallas kernels, shards(): pl.pallas_call(kernel, out_shape=(jax.ShapeDtypeStruct((ROWS, D), BF16),...  85.4 us
    unnamed x11, local copies, waits for them, and re-layouts  7.39 us

profile of v1, /device:TPU:6, one launch (start us, length us, event | category | flops | bytes accessed | tf_op | source)
XLA Modules:
  0.0 93.4 jit_solution(14484610390602808672)
XLA Ops:
  0.6 85.4 %shard_map.128 = (bf16[64,2048]{1,0:T(8,128)(2,1)}, bf16[1,2048,512]{2,1,0:T(8,128)(2,1)}, bf16[1,512,2048]{2,1,0:T(8,128)(2,1)}, f32[1,2048]{1,0:T(1,128)}, f32[1,2048]{1,0:T(1,128)}) custom-call(bf16[64,2048]{1,0:T(8,128)(2,1)} %tok.1, bf16[64,2048]{1,0:T(8,128)(2,1)} %cot.1, s32[1,64]{1,0:T(1,128)} %order.1, bf16[1,2048,512]{2,1,0:T(8,128)(2,1)} %win_h.1, ...), custom_call_target="tpu_custom_call" | custom-call | tf_op jit(solution)/shard_map/pallas_call | solution.py:432
  86.0 1.7 %copy.19 = bf16[64,2048]{1,0:T(8,128)(2,1)} copy(bf16[64,2048]{1,0:T(8,128)(2,1)} %get-tuple-element.10) | data formatting | bytes 524288
  87.7 0.0 copy-start
  87.7 3.2 %copy.20 = bf16[1,2048,512]{2,1,0:T(8,128)(2,1)} copy(bf16[1,2048,512]{2,1,0:T(8,128)(2,1)} %get-tuple-element.11) | data formatting | bytes 4194304
  90.9 0.0 copy-done
  90.9 0.0 copy-start.2
  90.9 0.0 copy-start.1
  90.9 1.3 %copy.21 = bf16[1,512,2048]{2,1,0:T(8,128)(2,1)} copy(bf16[1,512,2048]{2,1,0:T(8,128)(2,1)S(1)} %copy-done) | data formatting | bytes 4194304
  92.2 0.0 copy-done.2
  92.2 0.6 copy.22
  92.8 0.0 copy-done.1
  92.8 0.6 copy.23
Async XLA Ops:
  87.7 3.2 %copy-start = (bf16[1,512,2048]{2,1,0:T(8,128)(2,1)S(1)}, bf16[1,512,2048]{2,1,0:T(8,128)(2,1)}, u32[]{:S(2)}) copy-start(bf16[1,512,2048]{2,1,0:T(8,128)(2,1)} %get-tuple-element.12) | copy-start | bytes 6291460
  90.9 1.3 %copy-start.2 = (f32[1,2048]{1,0:T(1,128)S(1)}, f32[1,2048]{1,0:T(1,128)}, u32[]{:S(2)}) copy-start(f32[1,2048]{1,0:T(1,128)} %get-tuple-element.13) | copy-start | bytes 24580
  90.9 1.9 %copy-start.1 = (f32[1,2048]{1,0:T(1,128)S(1)}, f32[1,2048]{1,0:T(1,128)}, u32[]{:S(2)}) copy-start(f32[1,2048]{1,0:T(1,128)} %get-tuple-element.14) | copy-start | bytes 24580

commit v2 on v1

--- a/solution.py
+++ b/solution.py
@@ -16,6 +16,7 @@
 FD = 512
 CH = 512
 HALF = 32
+VMEM_BYTES = 44 * 2**20
 
 
 def dot_nn(a, b):
@@ -56,10 +57,10 @@
 
 def kernel(
     tok, cot, order, win_h, wout_h, gains, cent, pre_h, zout_h,
-    gt_o, gwi_o, gwo_o, gg_o, gc_o,
-    win, wout, pre, zout, act, slope, dh, dh2,
-    a_dy, a_x, r_dy, r_x, dy, x, part, rc, fa, fb, fc, fr1, fr2, stat, vec, dxs, rb, stage_i, stage_o,
-    load_sem, a2a_s, a2a_r, stat_s, stat_r, vec_s, vec_r, ret_s, ret_r, ag_s, ag_r, rs_s, rs_r, out_sem,
+    gt_o, gwi_o, gwo_o, vec_o,
+    win_t, wout_t, pre, zout, act, slope, dh,
+    a_dy, a_x, r_dy, r_x, dy, x, part, rc, fa, fb, fc, fr1, fr2, stat, vec, dxs, rb,
+    load_sem, a2a_s, a2a_r, stat_s, stat_r, vec_s, vec_r, ret_s, ret_r, ag_s, ag_r, rs_s, rs_r,
 ):
     e = lax.axis_index("expert")
     h = lax.axis_index("hidden")
@@ -86,8 +87,8 @@
         for k in range(4)
     ]
     loads.append(pltpu.make_async_copy(zout_h.at[0], zout, load_sem.at[4]))
-    loads.append(pltpu.make_async_copy(wout_h.at[0], wout, load_sem.at[5]))
-    loads.append(pltpu.make_async_copy(win_h.at[0], win, load_sem.at[6]))
+    loads.append(pltpu.make_async_copy(wout_h.at[0], gwo_o, load_sem.at[5]))
+    loads.append(pltpu.make_async_copy(win_h.at[0], gwi_o, load_sem.at[6]))
     for c in loads:
         c.start()
 
@@ -131,6 +132,11 @@
     dispatch(tok, a_x)
     a2a_start(1, a_x, r_x)
 
+    loads[5].wait()
+    wout_t[...] = gwo_o[...].T
+    loads[6].wait()
+    win_t[...] = gwi_o[...].T
+
     for k in range(4):
         loads[k].wait()
 
@@ -140,6 +146,8 @@
         a, g = gelu_pair(pre[k, rows].astype(F32))
         act[k, rows] = a.astype(BF16)
         slope[k, rows] = g
+
+    lo, hi = pl.ds(0, HALF), pl.ds(HALF, HALF)
 
     def remote(sems, i, src, dst, where):
         return pltpu.make_async_remote_copy(
@@ -149,17 +157,16 @@
 
     def gather_plan(t, buf):
         sems = (ag_s.at[t], ag_r.at[t])
-        lo, hi = pl.ds(0, HALF), pl.ds(HALF, HALF)
-        plan = {
-            "own_xp": (buf.at[0, yc], buf.at[3, yc], xp, buf.at[3, yc]),
-            "own_xm": (buf.at[0, yc], buf.at[1, yc], xm, buf.at[1, yc]),
-            "own_y": (buf.at[0, yc], buf.at[0, yc], yn, buf.at[0, yoc]),
-            "half_xp": (buf.at[3, yc, lo], buf.at[2, yc, lo], xp, buf.at[2, yc, lo]),
-            "half_xm": (buf.at[1, yc, hi], buf.at[2, yc, hi], xm, buf.at[2, yc, hi]),
-            "oy_xp": (buf.at[0, yoc], buf.at[3, yoc], xp, buf.at[3, yoc]),
-            "oy_xm": (buf.at[0, yoc], buf.at[1, yoc], xm, buf.at[1, yoc]),
-            "far_y": (buf.at[2, yc], buf.at[2, yc], yn, buf.at[2, yoc]),
-        }
+        plan = {}
+        for part_of, r in (("lo", lo), ("hi", hi)):
+            plan["own_xp_" + part_of] = (buf.at[0, yc, r], buf.at[3, yc, r], xp, buf.at[3, yc, r])
+            plan["own_xm_" + part_of] = (buf.at[0, yc, r], buf.at[1, yc, r], xm, buf.at[1, yc, r])
+            plan["own_y_" + part_of] = (buf.at[0, yc, r], buf.at[0, yc, r], yn, buf.at[0, yoc, r])
+            plan["oy_xp_" + part_of] = (buf.at[0, yoc, r], buf.at[3, yoc, r], xp, buf.at[3, yoc, r])
+            plan["oy_xm_" + part_of] = (buf.at[0, yoc, r], buf.at[1, yoc, r], xm, buf.at[1, yoc, r])
+            plan["far_y_" + part_of] = (buf.at[2, yc, r], buf.at[2, yc, r], yn, buf.at[2, yoc, r])
+        plan["half_xp"] = (buf.at[3, yc, lo], buf.at[2, yc, lo], xp, buf.at[2, yc, lo])
+        plan["half_xm"] = (buf.at[1, yc, hi], buf.at[2, yc, hi], xm, buf.at[2, yc, hi])
         for k in range(4):
             plan["core_%d" % k] = (buf.at[k, yc], buf.at[k, yc], cn, buf.at[k, 2 * yi + co])
             plan["core_y%d" % k] = (buf.at[k, yoc], buf.at[k, yoc], cn, buf.at[k, 2 * yo + co])
@@ -195,9 +202,100 @@
     gd = Gather(0, dy)
     gx = Gather(1, x)
 
+    def first_hop(g):
+        g.start("own_xp_lo", "own_xm_hi", "own_y_lo", "own_xp_hi", "own_xm_lo", "own_y_hi", "core_0")
+
+    def second_hop_a(g):
+        g.got("own_xp_lo")
+        g.start("half_xp")
+        g.got("own_xm_hi")
+        g.start("half_xm")
+
+    def second_hop_b(g):
+        g.got("own_y_lo")
+        g.start("oy_xp_lo", "oy_xm_lo")
+        g.got("own_y_hi")
+        g.start("oy_xp_hi", "oy_xm_hi", "core_y0")
+        g.got("own_xm_lo")
+        g.start("core_1")
+        g.got("own_xp_hi")
+        g.start("core_3")
+
+    def third_hop(g):
+        g.got("half_xp")
+        g.start("far_y_lo")
+        g.got("half_xm")
+        g.start("far_y_hi", "core_2")
+
+    def last_hop(g):
+        g.got("oy_xp_lo", "oy_xp_hi")
+        g.start("core_y3")
+        g.got("oy_xm_lo", "oy_xm_hi")
+        g.start("core_y1")
+
+    def last_far(g):
+        g.got("far_y_lo", "far_y_hi")
+        g.start("core_y2")
+
+    def forward(k, y):
+        rows = pl.ds(pl.multiple_of(y * 128, 128), 128)
+        acc = dot_nn(dy[k, pl.ds(2 * y, 2)].reshape(128, D), wout_t[...])
+        dh_rows = (acc * slope[k, rows]).astype(BF16)
+        dh[k, rows] = dh_rows
+        t = dot_nn(dh_rows, win_t[...]).astype(BF16)
+        part[0, k, y] = t[:ROWS]
+        part[1, k, y] = t[ROWS:]
+
+    rs_sems = (rs_s, rs_r)
+    core_rs = {}
+    for k in range(4):
+        core_rs[k, 0] = remote(rs_sems, 2 * k, part.at[co, k, yi], rc.at[k, yi], cn)
+        core_rs[k, 1] = remote(rs_sems, 2 * k + 1, part.at[co, k, yo], rc.at[k, yo], cn)
+
+    def forward_send(k, other):
+        forward(k, yo if other else yi)
+        core_rs[k, other].start()
+
+    def add(dst, *others):
+        total = dst[...].astype(F32)
+        for o in others:
+            total += o[...].astype(F32)
+        dst[...] = total.astype(BF16)
+
+    def both_cores(k, other):
+        core_rs[k, other].wait_recv()
+        y = yo if other else yi
+        add(part.at[ci, k, y], rc.at[k, y])
+
+    rs = {
+        "b_p": remote(rs_sems, 8, part.at[ci, 2, yi, lo], fb.at[0], xp),
+        "b_m": remote(rs_sems, 9, part.at[ci, 2, yi, hi], fb.at[1], xm),
+        "c_p": remote(rs_sems, 10, part.at[ci, 1, yi, lo], fc.at[0, lo], xp),
+        "c_m": remote(rs_sems, 11, part.at[ci, 3, yi, hi], fc.at[1, hi], xm),
+        "free_p": remote(rs_sems, 12, part.at[ci, 1, yi, hi], fc.at[0, hi], xp),
+        "free_m": remote(rs_sems, 13, part.at[ci, 3, yi, lo], fc.at[1, lo], xm),
+    }
+    for i, (part_of, r) in enumerate((("lo", lo), ("hi", hi))):
+        rs["a_p_" + part_of] = remote(rs_sems, 14 + 4 * i, part.at[ci, 1, yo, r], fa.at[0, r], xp)
+        rs["a_m_" + part_of] = remote(rs_sems, 15 + 4 * i, part.at[ci, 3, yo, r], fa.at[1, r], xm)
+        rs["r1_" + part_of] = remote(rs_sems, 16 + 4 * i, part.at[ci, 2, yo, r], fr1.at[r], yn)
+        rs["r2_" + part_of] = remote(rs_sems, 17 + 4 * i, part.at[ci, 0, yo, r], fr2.at[r], yn)
+
     a2a_arrived(0, a_dy, r_dy)
     collect(r_dy, dy)
-    gd.start("own_xp", "own_xm", "own_y", "core_0")
+    first_hop(gd)
+    gd.got("core_0")
+    forward_send(0, 0)
+    second_hop_a(gd)
+    second_hop_b(gd)
+    gd.got("core_1")
+    forward_send(1, 0)
+    both_cores(0, 0)
+    third_hop(gd)
+    gd.got("core_3")
+    forward_send(3, 0)
+    both_cores(1, 0)
+    rs["free_p"].start()
 
     a2a_arrived(1, a_x, r_x)
     collect(r_x, x)
@@ -212,7 +310,7 @@
     row_i, lane_i = iota((ROWS, 128), 0), iota((ROWS, 128), 1)
     s_mask, r_mask = lane_i == row_i, lane_i == row_i + ROWS
     stat[0, yc] = jnp.sum(jnp.where(s_mask, s, 0.0) + jnp.where(r_mask, r, 0.0), axis=0, keepdims=True)
-    vec[h, 1:2] = jnp.sum(dlogit * xf, axis=0, keepdims=True)
+    vec[h, 1] = jnp.sum(dlogit * xf, axis=0, keepdims=True)
 
     def stat_copy(i, got):
         to, frm = (h + i) % N, (h + N - i) % N
@@ -226,131 +324,85 @@
     def _(i):
         stat_copy(i, False).start()
 
-    gd.got("own_xp", "own_xm", "own_y")
-    gd.start("half_xp", "half_xm", "oy_xp", "oy_xm", "core_1", "core_3", "core_y0")
+    both_cores(3, 0)
+    rs["free_m"].start()
+    gd.got("core_y0")
+    forward_send(0, 1)
+    gd.got("core_2")
+    forward_send(2, 0)
+    last_hop(gd)
+    first_hop(gx)
+    last_far(gd)
+    gd.got("core_y1")
+    forward_send(1, 1)
+    gd.got("core_y3")
+    forward_send(3, 1)
+    both_cores(1, 1)
+    rs["a_p_lo"].start()
+    rs["a_p_hi"].start()
+    gd.got("core_y2")
+    forward_send(2, 1)
+    both_cores(3, 1)
+    rs["a_m_lo"].start()
+    rs["a_m_hi"].start()
+    both_cores(2, 1)
+    rs["r1_lo"].start()
+    rs["r1_hi"].start()
+    both_cores(2, 0)
+    both_cores(0, 1)
 
     @pl.loop(1, N)
     def _(i):
         stat_copy(i, True).wait()
 
-    loads[5].wait()
-    loads[6].wait()
-
-    def forward(k):
-        acc = [dot_nt(dy[k].reshape(256, D), wout[f * 256 : (f + 1) * 256]) for f in range(2)]
-        for j in range(4):
-            rows = slice(j * ROWS, (j + 1) * ROWS)
-            line = stat[k, j]
-            sj = jnp.sum(jnp.where(s_mask, line, 0.0), axis=1, keepdims=True)
-            rj = jnp.sum(jnp.where(r_mask, line, 0.0), axis=1, keepdims=True)
-            for f in range(2):
-                cols = slice(f * 256, (f + 1) * 256)
-                v = acc[f][rows] * (slope[k, rows, cols] * sj)
-                dh[k, rows, cols] = v.astype(BF16)
-                dh2[k, rows, cols] = (v * rj).astype(BF16)
-                act[k, rows, cols] = (act[k, rows, cols].astype(F32) * sj).astype(BF16)
-
-        @pl.loop(0, 8)
-        def _(n):
-            cols = pl.ds(pl.multiple_of(n * 256, 256), 256)
-            t = dot_nt(dh[k], win[cols]).astype(BF16)
-            for j in range(4):
-                part[j % 2, k, j // 2, :, cols] = t[j * ROWS : (j + 1) * ROWS]
-
-    rs_sems = (rs_s, rs_r)
-    core_rs = [remote(rs_sems, k, part.at[co, k], rc.at[k], cn) for k in range(4)]
-
-    gd.got("core_0", "core_y0")
-    forward(0)
-    core_rs[0].start()
-    gd.got("half_xp", "half_xm")
-    gd.start("far_y", "core_2")
-    gd.got("oy_xp", "oy_xm")
-    gd.start("core_y1", "core_y3")
-    gd.got("far_y")
-    gd.start("core_y2")
-    gx.start("own_xp", "own_xm", "own_y", "core_0")
-    gd.got("core_1", "core_y1")
-    forward(1)
-    core_rs[1].start()
-    gd.got("core_3", "core_y3")
-    forward(3)
-    core_rs[3].start()
-    gd.got("core_2", "core_y2")
-    forward(2)
-    core_rs[2].start()
-
-    def add(dst, *others):
-        total = dst[...].astype(F32)
-        for o in others:
-            total += o[...].astype(F32)
-        dst[...] = total.astype(BF16)
-
-    def both_cores(k):
-        core_rs[k].wait_recv()
-        add(part.at[ci, k], rc.at[k])
-
-    rs = {
-        "a_p": remote(rs_sems, 4, part.at[ci, 1, yo], fa.at[0], xp),
-        "a_m": remote(rs_sems, 5, part.at[ci, 3, yo], fa.at[1], xm),
-        "r1": remote(rs_sems, 6, part.at[ci, 2, yo], fr1, yn),
-        "b_p": remote(rs_sems, 7, part.at[ci, 2, yi, pl.ds(0, HALF)], fb.at[0], xp),
-        "b_m": remote(rs_sems, 8, part.at[ci, 2, yi, pl.ds(HALF, HALF)], fb.at[1], xm),
-        "r2": remote(rs_sems, 9, part.at[ci, 0, yo], fr2, yn),
-        "c_p": remote(rs_sems, 10, part.at[ci, 1, yi], fc.at[0], xp),
-        "c_m": remote(rs_sems, 11, part.at[ci, 3, yi], fc.at[1], xm),
-    }
-    both_cores(1)
-    rs["a_p"].start()
-    both_cores(3)
-    rs["a_m"].start()
-    both_cores(2)
-    rs["r1"].start()
-    both_cores(0)
-    gx.got("own_xp", "own_xm", "own_y")
-    gx.start("half_xp", "half_xm", "core_1", "core_3", "core_y0")
-
-    out_copies = []
+    @pl.loop(0, 16)
+    def _(i):
+        k, j = i // 4, i % 4
+        rows = pl.ds(pl.multiple_of(j * ROWS, ROWS), ROWS)
+        line = stat[k, j]
+        sj = jnp.sum(jnp.where(s_mask, line, 0.0), axis=1, keepdims=True)
+        rj = jnp.sum(jnp.where(r_mask, line, 0.0), axis=1, keepdims=True)
+        act[k, rows] = (act[k, rows].astype(F32) * sj).astype(BF16)
+        dh[k, rows] = (dh[k, rows].astype(F32) * (sj * rj)).astype(BF16)
 
     def weight_out(n):
-        cols = slice(n * 512, (n + 1) * 512)
-        stage_o[:, cols] = dot_tn(
-            act[...].reshape(N * ROWS, FD), dy[:, :, :, cols].reshape(N * ROWS, 512)
+        cols = slice(n * 1024, (n + 1) * 1024)
+        gwo_o[:, cols] = dot_tn(
+            act[...].reshape(N * ROWS, FD), dy[:, :, :, cols].reshape(N * ROWS, 1024)
         ).astype(BF16)
 
-    for n in range(4):
-        weight_out(n)
-    out_copies.append(pltpu.make_async_copy(stage_o, gwo_o.at[0], out_sem.at[0]))
-    out_copies[-1].start()
-
-    rs["r1"].wait_recv()
-    add(part.at[ci, 2, yi], fr1)
+    rs["r1_lo"].wait_recv()
+    add(part.at[ci, 2, yi, lo], fr1.at[lo])
     rs["b_p"].start()
+    rs["r1_hi"].wait_recv()
+    add(part.at[ci, 2, yi, hi], fr1.at[hi])
     rs["b_m"].start()
-    rs["a_p"].wait_recv()
-    rs["a_m"].wait_recv()
-    add(part.at[ci, 0, yo], fa.at[0], fa.at[1])
-    rs["r2"].start()
+    second_hop_a(gx)
+    for part_of, half in (("lo", lo), ("hi", hi)):
+        rs["a_p_" + part_of].wait_recv()
+        rs["a_m_" + part_of].wait_recv()
+        add(part.at[ci, 0, yo, half], fa.at[0, half], fa.at[1, half])
+        rs["r2_" + part_of].start()
     rs["b_p"].wait_recv()
-    add(part.at[ci, 1, yi, pl.ds(0, HALF)], fb.at[0])
+    add(part.at[ci, 1, yi, lo], fb.at[0])
     rs["c_p"].start()
     rs["b_m"].wait_recv()
-    add(part.at[ci, 3, yi, pl.ds(HALF, HALF)], fb.at[1])
+    add(part.at[ci, 3, yi, hi], fb.at[1])
     rs["c_m"].start()
-    gx.start("oy_xp", "oy_xm")
-    gx.got("half_xp", "half_xm")
-    gx.start("far_y", "core_2")
-
-    rs["r2"].wait_recv()
-    rs["c_p"].wait_recv()
-    rs["c_m"].wait_recv()
-    dn = (
+    second_hop_b(gx)
+    third_hop(gx)
+    weight_out(0)
+    weight_out(1)
+
+    for n in ("r2_lo", "r2_hi", "c_p", "c_m", "free_p", "free_m"):
+        rs[n].wait_recv()
+    dn = s * (
         part[ci, 0, yi].astype(F32) + fr2[...].astype(F32) + fc[0].astype(F32) + fc[1].astype(F32)
     )
     xf = x[0, yc].astype(F32)
     dyf = dy[0, yc].astype(F32)
     xhat = xf * r
-    vec[h, 0:1] = jnp.sum(dn * xhat, axis=0, keepdims=True)
+    vec[h, 0] = jnp.sum(dn * xhat, axis=0, keepdims=True)
     qv = dn * gains[...]
     m = jnp.sum(qv * xhat, axis=1, keepdims=True) * (1.0 / D)
     dx = (dyf * (1.0 + s) + r * (qv - xhat * m) + dlogit * cent[...]).astype(BF16)
@@ -382,20 +434,16 @@
 
     rb[e] = dxs[e]
 
-    gx.got("oy_xp", "oy_xm")
-    gx.start("core_y1", "core_y3")
-    gx.got("far_y")
-    gx.start("core_y2")
+    last_hop(gx)
+    last_far(gx)
     gx.got(*["core_%d" % k for k in range(4)], *["core_y%d" % k for k in range(4)])
 
     eye = iota((256, 256), 0) == iota((256, 256), 1)
     for n in range(8):
         cols = slice(n * 256, (n + 1) * 256)
         gain = jnp.sum(jnp.where(eye, gains[:, cols], 0.0), axis=1, keepdims=True)
-        t = dot_tn(x[:, :, :, cols].reshape(N * ROWS, 256), dh2[...].reshape(N * ROWS, FD))
-        stage_i[cols] = (t * gain).astype(BF16)
-    out_copies.append(pltpu.make_async_copy(stage_i, gwi_o.at[0], out_sem.at[1]))
-    out_copies[-1].start()
+        t = dot_tn(x[:, :, :, cols].reshape(N * ROWS, 256), dh[...].reshape(N * ROWS, FD))
+        gwi_o[cols] = (t * gain).astype(BF16)
 
     @pl.loop(1, N)
     def _(i):
@@ -411,43 +459,47 @@
     total = vec[0]
     for i in range(1, N):
         total += vec[i]
-    gg_o[...] = total[0:1]
-    gc_o[...] = total[1:2]
+    vec_o[...] = total
 
     gd.sent_all()
     gx.sent_all()
-    for c in core_rs:
+    for c in (*core_rs.values(), *rs.values()):
         c.wait_send()
-    for c in rs.values():
-        c.wait_send()
-    for c in out_copies:
+
+
+def write_out(gt, gwi, gwo, vec, gt_o, gwi_o, gwo_o, gg_o, gc_o, sem):
+    pairs = ((gwi, gwi_o.at[0]), (gwo, gwo_o.at[0]), (gt, gt_o), (vec.at[0], gg_o), (vec.at[1], gc_o))
+    copies = [pltpu.make_async_copy(a, b, sem.at[i]) for i, (a, b) in enumerate(pairs)]
+    for c in copies:
+        c.start()
+    for c in copies:
         c.wait()
 
 
 def shards(*args):
     vm = pl.BlockSpec(memory_space=pltpu.VMEM)
-    hbm = pl.BlockSpec(memory_space=pl.ANY)
+    hbm = pl.BlockSpec(memory_space=pltpu.HBM)
+    anywhere = pl.BlockSpec(memory_space=pl.ANY)
     rows4 = (4, 4, ROWS, D)
     dma = pltpu.SemaphoreType.DMA
-    return pl.pallas_call(
+    args = [pltpu.with_memory_space_constraint(a, pltpu.HBM) for a in args]
+    results = pl.pallas_call(
         kernel,
         out_shape=(
-            jax.ShapeDtypeStruct((ROWS, D), BF16),
-            jax.ShapeDtypeStruct((1, D, FD), BF16),
-            jax.ShapeDtypeStruct((1, FD, D), BF16),
-            jax.ShapeDtypeStruct((1, D), F32),
-            jax.ShapeDtypeStruct((1, D), F32),
+            pltpu.VMEM((ROWS, D), BF16),
+            pltpu.VMEM((D, FD), BF16),
+            pltpu.VMEM((FD, D), BF16),
+            pltpu.VMEM((2, 1, D), F32),
         ),
         in_specs=[vm, vm, vm, hbm, hbm, vm, vm, hbm, hbm],
-        out_specs=(vm, hbm, hbm, vm, vm),
+        out_specs=(vm,) * 4,
         scratch_shapes=[
+            pltpu.VMEM((FD, D), BF16),
             pltpu.VMEM((D, FD), BF16),
-            pltpu.VMEM((FD, D), BF16),
             pltpu.VMEM((4, 256, FD), BF16),
             pltpu.VMEM((ROWS, D), BF16),
             pltpu.VMEM((4, 256, FD), BF16),
             pltpu.VMEM((4, 256, FD), F32),
-            pltpu.VMEM((4, 256, FD), BF16),
             pltpu.VMEM((4, 256, FD), BF16),
             pltpu.VMEM((N, 16, CH), BF16),
             pltpu.VMEM((N, 16, CH), BF16),
@@ -463,24 +515,35 @@
             pltpu.VMEM((ROWS, D), BF16),
             pltpu.VMEM((ROWS, D), BF16),
             pltpu.VMEM((4, 4, 1, 128), F32),
-            pltpu.VMEM((N, 2, D), F32),
+            pltpu.VMEM((N, 2, 1, D), F32),
             pltpu.VMEM((N, 16, CH), BF16),
             pltpu.VMEM((N, 16, CH), BF16),
-            pltpu.VMEM((D, FD), BF16),
-            pltpu.VMEM((FD, D), BF16),
             dma((7,)),
             dma((2, N)), dma((2, N)),
             dma((N,)), dma((N,)),
             dma((N,)), dma((N,)),
             dma((N,)), dma((N,)),
-            dma((2, 16)), dma((2, 16)),
-            dma((12,)), dma((12,)),
-            dma((2,)),
+            dma((2, 22)), dma((2, 22)),
+            dma((22,)), dma((22,)),
         ],
         compiler_params=pltpu.CompilerParams(
-            collective_id=0, has_side_effects=True, vmem_limit_bytes=56 * 2**20
+            collective_id=0, has_side_effects=True, vmem_limit_bytes=VMEM_BYTES
         ),
     )(*args)
+    return pl.pallas_call(
+        write_out,
+        out_shape=(
+            jax.ShapeDtypeStruct((ROWS, D), BF16),
+            jax.ShapeDtypeStruct((1, D, FD), BF16),
+            jax.ShapeDtypeStruct((1, FD, D), BF16),
+            jax.ShapeDtypeStruct((1, D), F32),
+            jax.ShapeDtypeStruct((1, D), F32),
+        ),
+        in_specs=[anywhere] * 4,
+        out_specs=(hbm,) * 5,
+        scratch_shapes=[dma((5,))],
+        compiler_params=pltpu.CompilerParams(vmem_limit_bytes=2**20),
+    )(*results)
 
 
 def solution(mesh):

time: 94.2 us -> 78.7 us (0.84)
  Pallas kernels: 85.4 us -> 77.8 us
  local copies, waits for them, and re-layouts: 7.39 us -> 0 us
    pallas_call x1 -> x2, Pallas kernels: 85.4 us -> 77.8 us  [the longest x1 75.7 us: shards(): pl.pallas_call(kernel, out_shape=(pltpu.VMEM((ROWS, D), BF16), pltpu.VMEM...]
    unnamed x11 -> x0, local copies, waits for them, and re-layouts: 7.39 us -> none
where the time goes in v2:
time: 78.7 us; the launch traced here: 78.6 us
  Pallas kernels  77.8 us (99%)
  between operations  0.8 us (1%)
    pallas_call x1, Pallas kernels, shards(): pl.pallas_call(kernel, out_shape=(pltpu.VMEM((ROWS, D), BF16), pltpu.VMEM...  75.7 us
    pallas_call x1, Pallas kernels, shards(): pl.pallas_call(write_out, out_shape=(jax.ShapeDtypeStruct((ROWS, D), BF16...  2.13 us

profile of v2, /device:TPU:6, one launch (start us, length us, event | category | flops | bytes accessed | tf_op | source)
XLA Modules:
  0.0 78.6 jit_solution(10225586246892250137)
XLA Ops:
  0.6 75.7 %shard_map.128 = (bf16[64,2048]{1,0:T(8,128)(2,1)S(1)}, bf16[2048,512]{1,0:T(8,128)(2,1)S(1)}, bf16[512,2048]{1,0:T(8,128)(2,1)S(1)}, f32[2,1,2048]{2,1,0:T(1,128)S(1)}) custom-call(bf16[64,2048]{1,0:T(8,128)(2,1)} %tok.1, bf16[64,2048]{1,0:T(8,128)(2,1)} %cot.1, s32[1,64]{1,0:T(1,128)} %order.1, bf16[1,2048,512]{2,1,0:T(8,128)(2,1)} %win_h.1, ...), custom_call_target="tpu_custom_call" | custom-call | tf_op jit(solution)/shard_map/pallas_call | solution.py:486
  76.3 2.1 %shard_map.129 = (bf16[64,2048]{1,0:T(8,128)(2,1)}, bf16[1,2048,512]{2,1,0:T(8,128)(2,1)}, bf16[1,512,2048]{2,1,0:T(8,128)(2,1)}, f32[1,2048]{1,0:T(1,128)}, f32[1,2048]{1,0:T(1,128)}) custom-call(bf16[64,2048]{1,0:T(8,128)(2,1)S(1)} %get-tuple-element.9.gt, bf16[2048,512]{1,0:T(8,128)(2,1)S(1)} %get-tuple-element.10.gwi, ...), custom_call_target="tpu_custom_call" | custom-call | tf_op jit(solution)/shard_map/pallas_call | solution.py:533

commit v3 on v2

--- a/solution.py
+++ b/solution.py
@@ -56,11 +56,11 @@
 
 
 def kernel(
-    tok, cot, order, win_h, wout_h, gains, cent, pre_h, zout_h,
+    tok_h, cot_h, order_h, win_h, wout_h, gains_h, cent_h, pre_h, zout_h,
     gt_o, gwi_o, gwo_o, vec_o,
-    win_t, wout_t, pre, zout, act, slope, dh,
-    a_dy, a_x, r_dy, r_x, dy, x, part, rc, fa, fb, fc, fr1, fr2, stat, vec, dxs, rb,
-    load_sem, a2a_s, a2a_r, stat_s, stat_r, vec_s, vec_r, ret_s, ret_r, ag_s, ag_r, rs_s, rs_r,
+    tok, cot, order, gains, cent, win_t, wout_t, pre, pre_s, zout, act, slope, slope_s, dh, dh_s,
+    a_dy, a_x, r_dy, r_x, dy, x, part, fa, fb, fc, fr1, fr2, stat, vec, dxs, rb,
+    load_sem, a2a_s, a2a_r, stat_s, stat_r, vec_s, vec_r, ret_s, ret_r, ag_s, ag_r, rs_s, rs_r, pair_s, pair_r,
 ):
     e = lax.axis_index("expert")
     h = lax.axis_index("hidden")
@@ -82,16 +82,14 @@
         pl.semaphore_signal(barrier, 1, device_id={"expert": (e + i) % N, "hidden": h}, device_id_type=MESH)
         pl.semaphore_signal(barrier, 1, device_id={"expert": e, "hidden": (h + i) % N}, device_id_type=MESH)
 
-    loads = [
-        pltpu.make_async_copy(pre_h.at[0, pl.ds(pl.multiple_of(((xi + k) % 4) * 256, 256), 256)], pre.at[k], load_sem.at[k])
-        for k in range(4)
-    ]
-    loads.append(pltpu.make_async_copy(zout_h.at[0], zout, load_sem.at[4]))
-    loads.append(pltpu.make_async_copy(wout_h.at[0], gwo_o, load_sem.at[5]))
-    loads.append(pltpu.make_async_copy(win_h.at[0], gwi_o, load_sem.at[6]))
+    sources = [(order_h, order), (cot_h, cot), (tok_h, tok), (wout_h.at[0], gwo_o), (win_h.at[0], gwi_o)]
+    sources += [(pre_h.at[0, pl.ds(pl.multiple_of(((xi + k) % 4) * 256, 256), 256)], pre.at[k]) for k in range(4)]
+    sources += [(cent_h, cent), (gains_h, gains), (zout_h.at[0], zout)]
+    loads = [pltpu.make_async_copy(src, dst, load_sem.at[i]) for i, (src, dst) in enumerate(sources)]
     for c in loads:
         c.start()
 
+    loads[0].wait()
     to_slot = onehot(iota((ROWS, ROWS), 0) == order[...])
     q = iota((256, ROWS), 0)
     spread = onehot(iota((256, ROWS), 1) == ((q >> 4) << 2) + (q & 3))
@@ -126,26 +124,13 @@
                 device_id={"expert": (e + i) % N, "hidden": h}, device_id_type=MESH,
             ).wait()
 
+    loads[1].wait()
     dispatch(cot, a_dy)
     pl.semaphore_wait(barrier, 2 * (N - 1))
     a2a_start(0, a_dy, r_dy)
+    loads[2].wait()
     dispatch(tok, a_x)
     a2a_start(1, a_x, r_x)
-
-    loads[5].wait()
-    wout_t[...] = gwo_o[...].T
-    loads[6].wait()
-    win_t[...] = gwi_o[...].T
-
-    for k in range(4):
-        loads[k].wait()
-
-    @pl.loop(0, 16)
-    def _(i):
-        k, rows = i // 4, pl.ds(pl.multiple_of((i % 4) * 64, 64), 64)
-        a, g = gelu_pair(pre[k, rows].astype(F32))
-        act[k, rows] = a.astype(BF16)
-        slope[k, rows] = g
 
     lo, hi = pl.ds(0, HALF), pl.ds(HALF, HALF)
 
@@ -154,6 +139,33 @@
             src_ref=src, dst_ref=dst, send_sem=sems[0].at[i], recv_sem=sems[1].at[i],
             device_id={"expert": e, "hidden": where}, device_id_type=MESH,
         )
+
+    pair_sems = (pair_s, pair_r)
+    blocks = [(k, y) for k in range(4) for y in range(2)]
+
+    def rows_of(y, c):
+        return pl.ds(pl.multiple_of((2 * y + c) * ROWS, ROWS), ROWS)
+
+    pair = [remote(pair_sems, i, pre.at[k, rows_of(y, co)], pre_s.at[k, y], cn) for i, (k, y) in enumerate(blocks)]
+    pair.append(remote(pair_sems, 8, wout_t.at[0], wout_t.at[1], cn))
+    pair.append(remote(pair_sems, 9, win_t.at[0], win_t.at[1], cn))
+    loads[3].wait()
+    wout_t[0] = gwo_o[...].T
+    pair[8].start()
+    for k in range(4):
+        loads[5 + k].wait()
+    for c in pair[:8]:
+        c.start()
+    loads[4].wait()
+    win_t[0] = gwi_o[...].T
+    pair[9].start()
+
+    @pl.loop(0, 16)
+    def _(i):
+        k, rows = i // 4, pl.ds(pl.multiple_of((i % 4) * ROWS, ROWS), ROWS)
+        a, g = gelu_pair(pre[k, rows].astype(F32))
+        act[k, rows] = a.astype(BF16)
+        slope[k, rows] = g
 
     def gather_plan(t, buf):
         sems = (ag_s.at[t], ag_r.at[t])
@@ -202,8 +214,11 @@
     gd = Gather(0, dy)
     gx = Gather(1, x)
 
-    def first_hop(g):
-        g.start("own_xp_lo", "own_xm_hi", "own_y_lo", "own_xp_hi", "own_xm_lo", "own_y_hi", "core_0")
+    def first_hop_x(g):
+        g.start("own_xp_lo", "own_xm_hi", "own_xp_hi", "own_xm_lo", "core_0")
+
+    def first_hop_y(g):
+        g.start("own_y_lo", "own_y_hi")
 
     def second_hop_a(g):
         g.got("own_xp_lo")
@@ -216,6 +231,8 @@
         g.start("oy_xp_lo", "oy_xm_lo")
         g.got("own_y_hi")
         g.start("oy_xp_hi", "oy_xm_hi", "core_y0")
+
+    def first_cores(g):
         g.got("own_xm_lo")
         g.start("core_1")
         g.got("own_xp_hi")
@@ -237,24 +254,31 @@
         g.got("far_y_lo", "far_y_hi")
         g.start("core_y2")
 
-    def forward(k, y):
-        rows = pl.ds(pl.multiple_of(y * 128, 128), 128)
-        acc = dot_nn(dy[k, pl.ds(2 * y, 2)].reshape(128, D), wout_t[...])
-        dh_rows = (acc * slope[k, rows]).astype(BF16)
-        dh[k, rows] = dh_rows
-        t = dot_nn(dh_rows, win_t[...]).astype(BF16)
-        part[0, k, y] = t[:ROWS]
-        part[1, k, y] = t[ROWS:]
-
     rs_sems = (rs_s, rs_r)
-    core_rs = {}
+    dh_copies = {}
     for k in range(4):
-        core_rs[k, 0] = remote(rs_sems, 2 * k, part.at[co, k, yi], rc.at[k, yi], cn)
-        core_rs[k, 1] = remote(rs_sems, 2 * k + 1, part.at[co, k, yo], rc.at[k, yo], cn)
-
-    def forward_send(k, other):
-        forward(k, yo if other else yi)
-        core_rs[k, other].start()
+        for other, y in ((0, yi), (1, yo)):
+            dh_copies[k, other] = remote(rs_sems, 2 * k + other, dh_s.at[k, y], dh.at[k, rows_of(y, ci)], cn)
+
+    def forward(*shares):
+        at = [(k, yo if other else yi) for k, other in shares]
+        rows = [dy[k, 2 * y + ci] for k, y in at]
+        rows = jnp.concatenate(rows, axis=0) if len(rows) > 1 else rows[0]
+        mine, others = dot_nn(rows, wout_t[0]), dot_nn(rows, wout_t[1])
+        left, right = [], []
+        for i, (k, y) in enumerate(at):
+            cut = slice(i * ROWS, (i + 1) * ROWS)
+            left.append((mine[cut] * slope[k, rows_of(y, ci)]).astype(BF16))
+            right.append((others[cut] * slope_s[k, y]).astype(BF16))
+            dh[k, rows_of(y, ci)] = left[-1]
+            dh_s[k, y] = right[-1]
+        left = jnp.concatenate(left, axis=0) if len(at) > 1 else left[0]
+        right = jnp.concatenate(right, axis=0) if len(at) > 1 else right[0]
+        t = (dot_nn(left, win_t[0]) + dot_nn(right, win_t[1])).astype(BF16)
+        for i, (k, y) in enumerate(at):
+            part[k, y] = t[i * ROWS : (i + 1) * ROWS]
+        for share in shares:
+            dh_copies[share].start()
 
     def add(dst, *others):
         total = dst[...].astype(F32)
@@ -262,45 +286,45 @@
             total += o[...].astype(F32)
         dst[...] = total.astype(BF16)
 
-    def both_cores(k, other):
-        core_rs[k, other].wait_recv()
-        y = yo if other else yi
-        add(part.at[ci, k, y], rc.at[k, y])
-
     rs = {
-        "b_p": remote(rs_sems, 8, part.at[ci, 2, yi, lo], fb.at[0], xp),
-        "b_m": remote(rs_sems, 9, part.at[ci, 2, yi, hi], fb.at[1], xm),
-        "c_p": remote(rs_sems, 10, part.at[ci, 1, yi, lo], fc.at[0, lo], xp),
-        "c_m": remote(rs_sems, 11, part.at[ci, 3, yi, hi], fc.at[1, hi], xm),
-        "free_p": remote(rs_sems, 12, part.at[ci, 1, yi, hi], fc.at[0, hi], xp),
-        "free_m": remote(rs_sems, 13, part.at[ci, 3, yi, lo], fc.at[1, lo], xm),
+        "b_p": remote(rs_sems, 8, part.at[2, yi, lo], fb.at[0], xp),
+        "b_m": remote(rs_sems, 9, part.at[2, yi, hi], fb.at[1], xm),
+        "c_p": remote(rs_sems, 10, part.at[1, yi, lo], fc.at[0, lo], xp),
+        "c_m": remote(rs_sems, 11, part.at[3, yi, hi], fc.at[1, hi], xm),
+        "free_p": remote(rs_sems, 12, part.at[1, yi, hi], fc.at[0, hi], xp),
+        "free_m": remote(rs_sems, 13, part.at[3, yi, lo], fc.at[1, lo], xm),
     }
     for i, (part_of, r) in enumerate((("lo", lo), ("hi", hi))):
-        rs["a_p_" + part_of] = remote(rs_sems, 14 + 4 * i, part.at[ci, 1, yo, r], fa.at[0, r], xp)
-        rs["a_m_" + part_of] = remote(rs_sems, 15 + 4 * i, part.at[ci, 3, yo, r], fa.at[1, r], xm)
-        rs["r1_" + part_of] = remote(rs_sems, 16 + 4 * i, part.at[ci, 2, yo, r], fr1.at[r], yn)
-        rs["r2_" + part_of] = remote(rs_sems, 17 + 4 * i, part.at[ci, 0, yo, r], fr2.at[r], yn)
+        rs["a_p_" + part_of] = remote(rs_sems, 14 + 4 * i, part.at[1, yo, r], fa.at[0, r], xp)
+        rs["a_m_" + part_of] = remote(rs_sems, 15 + 4 * i, part.at[3, yo, r], fa.at[1, r], xm)
+        rs["r1_" + part_of] = remote(rs_sems, 16 + 4 * i, part.at[2, yo, r], fr1.at[r], yn)
+        rs["r2_" + part_of] = remote(rs_sems, 17 + 4 * i, part.at[0, yo, r], fr2.at[r], yn)
 
     a2a_arrived(0, a_dy, r_dy)
     collect(r_dy, dy)
-    first_hop(gd)
-    gd.got("core_0")
-    forward_send(0, 0)
+    first_hop_x(gd)
+    first_hop_y(gd)
+    for c in pair:
+        c.wait_recv()
+
+    @pl.loop(0, 8)
+    def _(i):
+        slope_s[i // 2, i % 2] = gelu_pair(pre_s[i // 2, i % 2].astype(F32))[1]
+
     second_hop_a(gd)
     second_hop_b(gd)
-    gd.got("core_1")
-    forward_send(1, 0)
-    both_cores(0, 0)
-    third_hop(gd)
-    gd.got("core_3")
-    forward_send(3, 0)
-    both_cores(1, 0)
-    rs["free_p"].start()
-
     a2a_arrived(1, a_x, r_x)
     collect(r_x, x)
-
-    loads[4].wait()
+    first_hop_x(gx)
+    first_cores(gd)
+    forward((1, 0), (3, 0), (0, 0), (0, 1))
+    rs["free_p"].start()
+    rs["free_m"].start()
+    third_hop(gd)
+    first_hop_y(gx)
+
+    for c in loads[9:]:
+        c.wait()
     xf = x[0, yc].astype(F32)
     dyf = dy[0, yc].astype(F32)
     r = lax.rsqrt(jnp.sum(xf * xf, axis=1, keepdims=True) * (1.0 / D) + 1e-06)
@@ -324,32 +348,21 @@
     def _(i):
         stat_copy(i, False).start()
 
-    both_cores(3, 0)
-    rs["free_m"].start()
-    gd.got("core_y0")
-    forward_send(0, 1)
-    gd.got("core_2")
-    forward_send(2, 0)
+    forward((2, 0),)
     last_hop(gd)
-    first_hop(gx)
+    forward((1, 1), (3, 1))
+    second_hop_a(gx)
+    rs["a_p_lo"].start()
+    rs["a_m_lo"].start()
+    rs["a_p_hi"].start()
+    rs["a_m_hi"].start()
     last_far(gd)
-    gd.got("core_y1")
-    forward_send(1, 1)
-    gd.got("core_y3")
-    forward_send(3, 1)
-    both_cores(1, 1)
-    rs["a_p_lo"].start()
-    rs["a_p_hi"].start()
-    gd.got("core_y2")
-    forward_send(2, 1)
-    both_cores(3, 1)
-    rs["a_m_lo"].start()
-    rs["a_m_hi"].start()
-    both_cores(2, 1)
+    forward((2, 1),)
     rs["r1_lo"].start()
     rs["r1_hi"].start()
-    both_cores(2, 0)
-    both_cores(0, 1)
+    gd.got(*["core_%d" % k for k in range(4)], *["core_y%d" % k for k in range(4)])
+    for c in dh_copies.values():
+        c.wait_recv()
 
     @pl.loop(1, N)
     def _(i):
@@ -372,24 +385,27 @@
         ).astype(BF16)
 
     rs["r1_lo"].wait_recv()
-    add(part.at[ci, 2, yi, lo], fr1.at[lo])
+    add(part.at[2, yi, lo], fr1.at[lo])
     rs["b_p"].start()
     rs["r1_hi"].wait_recv()
-    add(part.at[ci, 2, yi, hi], fr1.at[hi])
+    add(part.at[2, yi, hi], fr1.at[hi])
     rs["b_m"].start()
-    second_hop_a(gx)
+    gx.got("own_y_lo")
+    gx.start("oy_xp_lo", "oy_xm_lo")
+    first_cores(gx)
     for part_of, half in (("lo", lo), ("hi", hi)):
         rs["a_p_" + part_of].wait_recv()
         rs["a_m_" + part_of].wait_recv()
-        add(part.at[ci, 0, yo, half], fa.at[0, half], fa.at[1, half])
+        add(part.at[0, yo, half], fa.at[0, half], fa.at[1, half])
         rs["r2_" + part_of].start()
     rs["b_p"].wait_recv()
-    add(part.at[ci, 1, yi, lo], fb.at[0])
+    add(part.at[1, yi, lo], fb.at[0])
     rs["c_p"].start()
     rs["b_m"].wait_recv()
-    add(part.at[ci, 3, yi, hi], fb.at[1])
+    add(part.at[3, yi, hi], fb.at[1])
     rs["c_m"].start()
-    second_hop_b(gx)
+    gx.got("own_y_hi")
+    gx.start("oy_xp_hi", "oy_xm_hi", "core_y0")
     third_hop(gx)
     weight_out(0)
     weight_out(1)
@@ -397,7 +413,7 @@
     for n in ("r2_lo", "r2_hi", "c_p", "c_m", "free_p", "free_m"):
         rs[n].wait_recv()
     dn = s * (
-        part[ci, 0, yi].astype(F32) + fr2[...].astype(F32) + fc[0].astype(F32) + fc[1].astype(F32)
+        part[0, yi].astype(F32) + fr2[...].astype(F32) + fc[0].astype(F32) + fc[1].astype(F32)
     )
     xf = x[0, yc].astype(F32)
     dyf = dy[0, yc].astype(F32)
@@ -447,8 +463,16 @@
 
     @pl.loop(1, N)
     def _(i):
+        vec_copy(i, True).wait()
+
+    total = vec[0]
+    for i in range(1, N):
+        total += vec[i]
+    vec_o[...] = total
+
+    @pl.loop(1, N)
+    def _(i):
         ret_copy(i, True).wait()
-        vec_copy(i, True).wait()
 
     back = rb[...].reshape(256, CH)
     slot_of = dot_nt(to_slot, spread)
@@ -456,14 +480,10 @@
     for c in range(4):
         w = jnp.where(((q2 >> 2) & 3) == c, slot_of, 0.0).astype(BF16)
         gt_o[:, c * CH : (c + 1) * CH] = dot_nn(w, back).astype(BF16)
-    total = vec[0]
-    for i in range(1, N):
-        total += vec[i]
-    vec_o[...] = total
 
     gd.sent_all()
     gx.sent_all()
-    for c in (*core_rs.values(), *rs.values()):
+    for c in (*pair, *dh_copies.values(), *rs.values()):
         c.wait_send()
 
 
@@ -491,23 +511,30 @@
             pltpu.VMEM((FD, D), BF16),
             pltpu.VMEM((2, 1, D), F32),
         ),
-        in_specs=[vm, vm, vm, hbm, hbm, vm, vm, hbm, hbm],
+        in_specs=[hbm] * 9,
         out_specs=(vm,) * 4,
         scratch_shapes=[
-            pltpu.VMEM((FD, D), BF16),
-            pltpu.VMEM((D, FD), BF16),
+            pltpu.VMEM((ROWS, D), BF16),
+            pltpu.VMEM((ROWS, D), BF16),
+            pltpu.VMEM((1, ROWS), jnp.int32),
+            pltpu.VMEM((1, D), F32),
+            pltpu.VMEM((1, D), F32),
+            pltpu.VMEM((2, FD, D), BF16),
+            pltpu.VMEM((2, D, FD), BF16),
             pltpu.VMEM((4, 256, FD), BF16),
+            pltpu.VMEM((4, 2, ROWS, FD), BF16),
             pltpu.VMEM((ROWS, D), BF16),
             pltpu.VMEM((4, 256, FD), BF16),
             pltpu.VMEM((4, 256, FD), F32),
+            pltpu.VMEM((4, 2, ROWS, FD), F32),
             pltpu.VMEM((4, 256, FD), BF16),
+            pltpu.VMEM((4, 2, ROWS, FD), BF16),
             pltpu.VMEM((N, 16, CH), BF16),
             pltpu.VMEM((N, 16, CH), BF16),
             pltpu.VMEM((N, 16, CH), BF16),
             pltpu.VMEM((N, 16, CH), BF16),
             pltpu.VMEM(rows4, BF16),
             pltpu.VMEM(rows4, BF16),
-            pltpu.VMEM((2, 4, 2, ROWS, D), BF16),
             pltpu.VMEM((4, 2, ROWS, D), BF16),
             pltpu.VMEM((2, ROWS, D), BF16),
             pltpu.VMEM((2, HALF, D), BF16),
@@ -518,13 +545,14 @@
             pltpu.VMEM((N, 2, 1, D), F32),
             pltpu.VMEM((N, 16, CH), BF16),
             pltpu.VMEM((N, 16, CH), BF16),
-            dma((7,)),
+            dma((12,)),
             dma((2, N)), dma((2, N)),
             dma((N,)), dma((N,)),
             dma((N,)), dma((N,)),
             dma((N,)), dma((N,)),
             dma((2, 22)), dma((2, 22)),
             dma((22,)), dma((22,)),
+            dma((10,)), dma((10,)),
         ],
         compiler_params=pltpu.CompilerParams(
             collective_id=0, has_side_effects=True, vmem_limit_bytes=VMEM_BYTES

time: 78.7 us -> 77.6 us (0.986); the launches traced: 78.6 us -> 76.2 us
  Pallas kernels: 77.8 us -> 75.4 us
    pallas_call x1, Pallas kernels: 75.7 us -> 73.2 us  [shards(): pl.pallas_call(kernel, out_shape=(pltpu.VMEM((ROWS, D), BF16), pltpu.VMEM...]
where the time goes in v3:
time: 77.6 us; the launch traced here: 76.2 us
  Pallas kernels  75.4 us (97%)
  between operations  0.8 us (1%)
    pallas_call x1, Pallas kernels, shards(): pl.pallas_call(kernel, out_shape=(pltpu.VMEM((ROWS, D), BF16), pltpu.VMEM...  73.2 us
    pallas_call x1, Pallas kernels, shards(): pl.pallas_call(write_out, out_shape=(jax.ShapeDtypeStruct((ROWS, D), BF16...  2.13 us

profile of v3, /device:TPU:6, one launch (start us, length us, event | category | flops | bytes accessed | tf_op | source)
XLA Modules:
  0.0 76.2 jit_solution(11079244382044691885)
XLA Ops:
  0.6 73.2 %shard_map.128 = (bf16[64,2048]{1,0:T(8,128)(2,1)S(1)}, bf16[2048,512]{1,0:T(8,128)(2,1)S(1)}, bf16[512,2048]{1,0:T(8,128)(2,1)S(1)}, f32[2,1,2048]{2,1,0:T(1,128)S(1)}) custom-call(bf16[64,2048]{1,0:T(8,128)(2,1)} %tok_h.1, bf16[64,2048]{1,0:T(8,128)(2,1)} %cot_h.1, s32[1,64]{1,0:T(1,128)} %order_h.1, bf16[1,2048,512]{2,1,0:T(8,128)(2,1)} %win_h.1, ...), custom_call_target="tpu_custom_call" | custom-call | tf_op jit(solution)/shard_map/pallas_call | solution.py:506
  73.9 2.1 %shard_map.129 = (bf16[64,2048]{1,0:T(8,128)(2,1)}, bf16[1,2048,512]{2,1,0:T(8,128)(2,1)}, bf16[1,512,2048]{2,1,0:T(8,128)(2,1)}, f32[1,2048]{1,0:T(1,128)}, f32[1,2048]{1,0:T(1,128)}) custom-call(bf16[64,2048]{1,0:T(8,128)(2,1)S(1)} %get-tuple-element.9.gt, bf16[2048,512]{1,0:T(8,128)(2,1)S(1)} %get-tuple-element.10.gwi, ...), custom_call_target="tpu_custom_call" | custom-call | tf_op jit(solution)/shard_map/pallas_call | solution.py:561

commit v4 on v3

--- a/solution.py
+++ b/solution.py
@@ -59,7 +59,7 @@
     tok_h, cot_h, order_h, win_h, wout_h, gains_h, cent_h, pre_h, zout_h,
     gt_o, gwi_o, gwo_o, vec_o,
     tok, cot, order, gains, cent, win_t, wout_t, pre, pre_s, zout, act, slope, slope_s, dh, dh_s,
-    a_dy, a_x, r_dy, r_x, dy, x, part, fa, fb, fc, fr1, fr2, stat, vec, dxs, rb,
+    a_dy, a_x, r_dy, r_x, dy, x, part, fa, fb, fc, fr1, fr2, stat, vec, dxs, rb, acc_i,
     load_sem, a2a_s, a2a_r, stat_s, stat_r, vec_s, vec_r, ret_s, ret_r, ag_s, ag_r, rs_s, rs_r, pair_s, pair_r,
 ):
     e = lax.axis_index("expert")
@@ -77,16 +77,19 @@
 
     barrier = pltpu.get_barrier_semaphore()
 
-    @pl.loop(1, N)
-    def _(i):
-        pl.semaphore_signal(barrier, 1, device_id={"expert": (e + i) % N, "hidden": h}, device_id_type=MESH)
-        pl.semaphore_signal(barrier, 1, device_id={"expert": e, "hidden": (h + i) % N}, device_id_type=MESH)
-
     sources = [(order_h, order), (cot_h, cot), (tok_h, tok), (wout_h.at[0], gwo_o), (win_h.at[0], gwi_o)]
     sources += [(pre_h.at[0, pl.ds(pl.multiple_of(((xi + k) % 4) * 256, 256), 256)], pre.at[k]) for k in range(4)]
     sources += [(cent_h, cent), (gains_h, gains), (zout_h.at[0], zout)]
     loads = [pltpu.make_async_copy(src, dst, load_sem.at[i]) for i, (src, dst) in enumerate(sources)]
-    for c in loads:
+    for c in loads[:2]:
+        c.start()
+
+    @pl.loop(1, N)
+    def _(i):
+        pl.semaphore_signal(barrier, 1, device_id={"expert": (e + i) % N, "hidden": h}, device_id_type=MESH)
+        pl.semaphore_signal(barrier, 1, device_id={"expert": e, "hidden": (h + i) % N}, device_id_type=MESH)
+
+    for c in loads[2:]:
         c.start()
 
     loads[0].wait()
@@ -390,8 +393,6 @@
     rs["r1_hi"].wait_recv()
     add(part.at[2, yi, hi], fr1.at[hi])
     rs["b_m"].start()
-    gx.got("own_y_lo")
-    gx.start("oy_xp_lo", "oy_xm_lo")
     first_cores(gx)
     for part_of, half in (("lo", lo), ("hi", hi)):
         rs["a_p_" + part_of].wait_recv()
@@ -404,11 +405,17 @@
     rs["b_m"].wait_recv()
     add(part.at[3, yi, hi], fb.at[1])
     rs["c_m"].start()
-    gx.got("own_y_hi")
-    gx.start("oy_xp_hi", "oy_xm_hi", "core_y0")
+    second_hop_b(gx)
     third_hop(gx)
     weight_out(0)
     weight_out(1)
+
+    gx.got("core_0", "core_1", "core_3", "core_y0")
+    right = jnp.concatenate([dh[0], *(dh[k, pl.ds(pl.multiple_of(128 * yi, 128), 128)] for k in (1, 3))], axis=0)
+    for n in range(8):
+        cols = slice(n * 256, (n + 1) * 256)
+        left = [x[0, :, :, cols].reshape(256, 256), *(x[k, pl.ds(2 * yi, 2), :, cols].reshape(128, 256) for k in (1, 3))]
+        acc_i[cols] = dot_tn(jnp.concatenate(left, axis=0), right)
 
     for n in ("r2_lo", "r2_hi", "c_p", "c_m", "free_p", "free_m"):
         rs[n].wait_recv()
@@ -452,13 +459,15 @@
 
     last_hop(gx)
     last_far(gx)
-    gx.got(*["core_%d" % k for k in range(4)], *["core_y%d" % k for k in range(4)])
+    gx.got("core_2", "core_y1", "core_y2", "core_y3")
 
     eye = iota((256, 256), 0) == iota((256, 256), 1)
+    right = jnp.concatenate([dh[2], *(dh[k, pl.ds(pl.multiple_of(128 * yo, 128), 128)] for k in (1, 3))], axis=0)
     for n in range(8):
         cols = slice(n * 256, (n + 1) * 256)
         gain = jnp.sum(jnp.where(eye, gains[:, cols], 0.0), axis=1, keepdims=True)
-        t = dot_tn(x[:, :, :, cols].reshape(N * ROWS, 256), dh[...].reshape(N * ROWS, FD))
+        left = [x[2, :, :, cols].reshape(256, 256), *(x[k, pl.ds(2 * yo, 2), :, cols].reshape(128, 256) for k in (1, 3))]
+        t = acc_i[cols] + dot_tn(jnp.concatenate(left, axis=0), right)
         gwi_o[cols] = (t * gain).astype(BF16)
 
     @pl.loop(1, N)
@@ -545,6 +554,7 @@
             pltpu.VMEM((N, 2, 1, D), F32),
             pltpu.VMEM((N, 16, CH), BF16),
             pltpu.VMEM((N, 16, CH), BF16),
+            pltpu.VMEM((D, FD), F32),
             dma((12,)),
             dma((2, N)), dma((2, N)),
             dma((N,)), dma((N,)),

time: 77.6 us -> 76.3 us (0.983)
  no operation moved by 1% of the time
where the time goes in v4:
time: 76.3 us; the launch traced here: 75.5 us
  Pallas kernels  74.9 us (98%)
    pallas_call x1, Pallas kernels, shards(): pl.pallas_call(kernel, out_shape=(pltpu.VMEM((ROWS, D), BF16), pltpu.VMEM...  72.8 us
    pallas_call x1, Pallas kernels, shards(): pl.pallas_call(write_out, out_shape=(jax.ShapeDtypeStruct((ROWS, D), BF16...  2.13 us

profile of v4, /device:TPU:6, one launch (start us, length us, event | category | flops | bytes accessed | tf_op | source)
XLA Modules:
  0.0 75.5 jit_solution(12204672685119122427)
XLA Ops:
  0.6 72.8 %shard_map.128 = (bf16[64,2048]{1,0:T(8,128)(2,1)S(1)}, bf16[2048,512]{1,0:T(8,128)(2,1)S(1)}, bf16[512,2048]{1,0:T(8,128)(2,1)S(1)}, f32[2,1,2048]{2,1,0:T(1,128)S(1)}) custom-call(bf16[64,2048]{1,0:T(8,128)(2,1)} %tok_h.1, bf16[64,2048]{1,0:T(8,128)(2,1)} %cot_h.1, s32[1,64]{1,0:T(1,128)} %order_h.1, bf16[1,2048,512]{2,1,0:T(8,128)(2,1)} %win_h.1, ...), custom_call_target="tpu_custom_call" | custom-call | tf_op jit(solution)/shard_map/pallas_call | solution.py:515
  73.4 2.1 %shard_map.129 = (bf16[64,2048]{1,0:T(8,128)(2,1)}, bf16[1,2048,512]{2,1,0:T(8,128)(2,1)}, bf16[1,512,2048]{2,1,0:T(8,128)(2,1)}, f32[1,2048]{1,0:T(1,128)}, f32[1,2048]{1,0:T(1,128)}) custom-call(bf16[64,2048]{1,0:T(8,128)(2,1)S(1)} %get-tuple-element.9.gt, bf16[2048,512]{1,0:T(8,128)(2,1)S(1)} %get-tuple-element.10.gwi, ...), custom_call_target="tpu_custom_call" | custom-call | tf_op jit(solution)/shard_map/pallas_call | solution.py:571

commit v5 on v4

--- a/solution.py
+++ b/solution.py
@@ -84,8 +84,7 @@
     for c in loads[:2]:
         c.start()
 
-    @pl.loop(1, N)
-    def _(i):
+    for i in range(1, N):
         pl.semaphore_signal(barrier, 1, device_id={"expert": (e + i) % N, "hidden": h}, device_id_type=MESH)
         pl.semaphore_signal(barrier, 1, device_id={"expert": e, "hidden": (h + i) % N}, device_id_type=MESH)
 

time: 76.3 us -> 76.3 us (level)
  no operation moved by 1% of the time
where the time goes in v5:
time: 76.3 us; the launch traced here: 75.8 us
  Pallas kernels  75.1 us (98%)
    pallas_call x1, Pallas kernels, shards(): pl.pallas_call(kernel, out_shape=(pltpu.VMEM((ROWS, D), BF16), pltpu.VMEM...  73 us
    pallas_call x1, Pallas kernels, shards(): pl.pallas_call(write_out, out_shape=(jax.ShapeDtypeStruct((ROWS, D), BF16...  2.13 us

profile of v5, /device:TPU:6, one launch (start us, length us, event | category | flops | bytes accessed | tf_op | source)
XLA Modules:
  0.0 75.8 jit_solution(5652774345668463460)
XLA Ops:
  0.6 73.0 %shard_map.128 = (bf16[64,2048]{1,0:T(8,128)(2,1)S(1)}, bf16[2048,512]{1,0:T(8,128)(2,1)S(1)}, bf16[512,2048]{1,0:T(8,128)(2,1)S(1)}, f32[2,1,2048]{2,1,0:T(1,128)S(1)}) custom-call(bf16[64,2048]{1,0:T(8,128)(2,1)} %tok_h.1, bf16[64,2048]{1,0:T(8,128)(2,1)} %cot_h.1, s32[1,64]{1,0:T(1,128)} %order_h.1, bf16[1,2048,512]{2,1,0:T(8,128)(2,1)} %win_h.1, ...), custom_call_target="tpu_custom_call" | custom-call | tf_op jit(solution)/shard_map/pallas_call | solution.py:514
  73.6 2.1 %shard_map.129 = (bf16[64,2048]{1,0:T(8,128)(2,1)}, bf16[1,2048,512]{2,1,0:T(8,128)(2,1)}, bf16[1,512,2048]{2,1,0:T(8,128)(2,1)}, f32[1,2048]{1,0:T(1,128)}, f32[1,2048]{1,0:T(1,128)}) custom-call(bf16[64,2048]{1,0:T(8,128)(2,1)S(1)} %get-tuple-element.9.gt, bf16[2048,512]{1,0:T(8,128)(2,1)S(1)} %get-tuple-element.10.gwi, ...), custom_call_target="tpu_custom_call" | custom-call | tf_op jit(solution)/shard_map/pallas_call | solution.py:570
